TPU v7x, 32 devices: a whole 2x2x4 slice. The times are simulated.
32 devices in a mesh: row: 2 (over y), col: 4 (over x, core), tok: 4 (over z).
Axes of the slice: x: 2, y: 2, z: 4, core: 2. Of those that a mesh axis runs over, the one named last changes fastest.
Arguments:
- first_inputs: bfloat16 [1024, 8192], P(('row', 'col'), 'tok'), may hold values from -12 to 12, as said below
- second_inputs: bfloat16 [1024, 8192], P(('row', 'col'), 'tok'), may hold values from -12 to 12, as said below
- first_weights: bfloat16 [8192, 2, 14336], P('tok', None, ('row', 'col')), may hold values from -0.0625 to 0.0625
- second_weights: bfloat16 [8192, 2, 14336], P('tok', None, ('col', 'row')), may hold values from -0.0625 to 0.0625
Outputs:
- unit_scores: float32 [14336, 14336], P(('row', 'tok'), 'col')
Inputs may be any that keep to these rules, and one draw needn't show every extreme that they name: `first_inputs`: the first model's layer input for each calibration token. `second_inputs`: the second model's layer input for each calibration token.
All inputs are finite; a program needn't handle non-finite values.
Results may differ from a plain program's by a relative error of at most 0.015.
Values may be sent and summed in bfloat16 or wider, within the bound.
A program may use at most 192 MiB of HBM per device.

v0:
```python
import jax
import jax.numpy as jnp
from jax import lax
from jax.sharding import PartitionSpec as P


def standardize(deviation, spread):
    return (deviation * lax.rsqrt(spread + 1e-05)).astype(jnp.bfloat16)


def local(first_inputs, second_inputs, first_weights, second_weights):
    full_first, full_second = (
        lax.all_gather(first_inputs, ("row", "col"), axis=0, tiled=True),
        lax.all_gather(second_inputs, ("row", "col"), axis=0, tiled=True),
    )
    width_local = first_weights.shape[0]
    count_first = first_weights.shape[2]
    count_second = second_weights.shape[2]
    matrix_first = first_weights.reshape(width_local, 2 * count_first)
    matrix_second = second_weights.reshape(width_local, 2 * count_second)
    depth = lax.axis_size("tok")
    tok_local = full_first.shape[0] // depth
    tokens_total = tok_local * depth
    term_first = jnp.dot(full_first, matrix_first, preferred_element_type=jnp.float32)
    term_second = jnp.dot(full_second, matrix_second, preferred_element_type=jnp.float32)
    summed = lax.psum_scatter(
        jnp.concatenate([term_first, term_second], axis=1), "tok", scatter_dimension=0, tiled=True
    )
    act_first = jax.nn.silu(summed[:, :count_first]) * summed[:, count_first : 2 * count_first]
    offset = 2 * count_first
    act_second = (
        jax.nn.silu(summed[:, offset : offset + count_second]) * summed[:, offset + count_second :]
    )
    inverse = 1.0 / tokens_total
    sum_first, sum_second = lax.psum(
        (jnp.sum(act_first, axis=0), jnp.sum(act_second, axis=0)), "tok"
    )
    dev_first = act_first - sum_first * inverse
    dev_second = act_second - sum_second * inverse
    square_first, square_second = lax.psum(
        (jnp.sum(dev_first * dev_first, axis=0), jnp.sum(dev_second * dev_second, axis=0)), "tok"
    )
    spread_first = square_first * inverse
    spread_second = square_second * inverse
    norm_first = standardize(dev_first, spread_first)
    norm_second = standardize(dev_second, spread_second)
    block_first = lax.all_gather(norm_first, "col", axis=1, tiled=True)
    block_second = lax.all_gather(norm_second, "row", axis=1, tiled=True)
    total = lax.psum_scatter(
        lax.dot_general(
            block_first, block_second, (((0,), (0,)), ((), ())), preferred_element_type=jnp.float32
        ).astype(jnp.bfloat16),
        "tok",
        scatter_dimension=0,
        tiled=True,
    ).astype(jnp.float32)
    return total * float(tokens_total) ** (-0.5)


def solution(mesh):
    placed = (
        P(("row", "col"), "tok"),
        P(("row", "col"), "tok"),
        P("tok", None, ("row", "col")),
        P("tok", None, ("col", "row")),
    )
    return jax.shard_map(
        local, mesh=mesh, in_specs=placed, out_specs=P(("row", "tok"), "col"), check_vma=False
    )
```

profile of v0, /device:TPU:0, one launch (start us, length us, event | category | flops | bytes accessed | tf_op | source)
XLA Modules:
  0.0 1598.7 jit_solution(12478790609891230202)
XLA Ops:
  6.5 0.0 all-gather.5.cloned.1.call-start
  6.5 0.7 all-gather.5.cloned.1.call-update
  7.3 0.0 all-gather.7.cloned.1.call-start
  7.3 0.0 slice-start
  7.3 0.7 all-gather.7.cloned.1.call-update
  8.0 0.0 reduce-scatter.3.cloned.1.call-start
  8.1 0.0 slice-start.1
  8.1 0.0 slice-start.2
  8.1 0.0 slice-start.3
  8.1 17.1 %copy.5 = bf16[256,8,2,1792]{3,1,2,0:T(8,128)(2,1)} copy(bf16[256,8,2,1792]{3,2,1,0:T(2,128)(2,1)} %bitcast.10) | data formatting | bytes 29360128
  25.2 0.0 slice-done
  25.2 0.0 slice-done.1
  25.2 0.0 slice-done.2
  25.2 0.0 slice-done.3
  25.2 7.1 copy.6
  32.3 16.3 %all-gather.5.cloned.1.call-done = bf16[1024,2048]{1,0:T(8,128)(2,1)} async-done(((bf16[128,2048]{1,0:T(8,128)(2,1)}), bf16[1024,2048]{1,0:T(8,128)(2,1)}) %all-gather.5.cloned.1.call-update) | async-done | bytes 4194320 | tf_op jit(solution)/shard_map/all_gather | solution.py:13
  48.7 22.8 %fusion.2 = f32[1024,3584]{1,0:T(8,128)} fusion(bf16[1024,2048]{1,0:T(8,128)(2,1)} %all-gather.5.cloned.1.call-done, bf16[2048,3584]{1,0:T(8,128)(2,1)} %bitcast.15), kind=kOutput, calls=%fused_computation.15 | convolution fusion | flops 15032385536 | bytes 33554432 | tf_op jit(solution)/shard_map/dot_general | solution.py:24
  71.5 15.8 all-gather.7.cloned.1.call-done
  87.3 0.0 copy-start
  87.3 23.1 %fusion.3 = f32[1024,3584]{1,0:T(8,128)} fusion(bf16[1024,2048]{1,0:T(8,128)(2,1)} %all-gather.7.cloned.1.call-done, bf16[2048,3584]{1,0:T(8,128)(2,1)} %bitcast.14), kind=kOutput, calls=%fused_computation.16 | convolution fusion | flops 15032385536 | bytes 33554432 | tf_op jit(solution)/shard_map/dot_general | solution.py:25
  110.5 0.0 copy-done
  110.5 18.4 %pad_maximum_fusion = f32[1024,7168]{1,0:T(8,128)} fusion(f32[1024,3584]{1,0:T(8,128)} %fusion.3, f32[1024,3584]{1,0:T(8,128)S(1)} %copy-done), kind=kLoop, calls=%fused_computation.1 | loop fusion | flops 7340032 | bytes 58720256 | tf_op jit(solution)/shard_map/concatenate | solution.py:27
  128.9 0.0 reduce-scatter.3.cloned.1.call-update
  128.9 0.0 all-gather.11.cloned.1.call-start
  129.0 481.7 %reduce-scatter.3.cloned.1.call-done = f32[256,7168]{1,0:T(8,128)} async-done(((f32[1024,7168]{1,0:T(8,128)}), f32[256,7168]{1,0:T(8,128)}) %reduce-scatter.3.cloned.1.call-update) | async-done | bytes 7340048 | tf_op jit(solution)/shard_map/reduce_scatter | solution.py:26
  610.7 5.4 fusion
  616.1 19.6 %all-reduce.1 = (f32[1792]{0:T(1024)S(1)}, f32[1792]{0:T(1024)S(1)}) all-reduce(f32[1792]{0:T(1024)S(1)} %get-tuple-element.13, f32[1792]{0:T(1024)S(1)} %get-tuple-element.9), channel_id=1, replica_groups=mesh['row'=2,'col'=4,'tok'=4] {'tok'}, use_global_device_ids=true, to_apply=%region_2.3 | all-reduce | flops 3584 | bytes 28672 | tf_op jit(solution)/shard_map/psum | solution.py:35
  635.6 1.9 multiply_reduce_fusion
  637.5 15.6 all-reduce
  653.1 2.6 multiply_convert_fusion
  655.7 0.0 all-gather.11.cloned.1.call-update
  655.8 0.0 all-gather.9.cloned.1.call-start
  655.8 1.1 multiply_convert_fusion.1
  656.9 0.0 all-gather.9.cloned.1.call-update
  656.9 0.0 reduce-scatter.5.cloned.1.call-start
  657.0 27.8 %all-gather.11.cloned.1.call-done = bf16[256,3584]{1,0:T(8,128)(2,1)} async-done(((bf16[256,1792]{1,0:T(8,128)(2,1)}), bf16[256,3584]{1,0:T(8,128)(2,1)}) %all-gather.11.cloned.1.call-update) | async-done | bytes 1835024 | tf_op jit(solution)/shard_map/all_gather | solution.py:48
  684.7 33.0 %all-gather.9.cloned.1.call-done = bf16[256,7168]{1,0:T(8,128)(2,1)} async-done(((bf16[256,1792]{1,0:T(8,128)(2,1)}), bf16[256,7168]{1,0:T(8,128)(2,1)}) %all-gather.9.cloned.1.call-update) | async-done | bytes 3670032 | tf_op jit(solution)/shard_map/all_gather | solution.py:47
  717.8 22.3 %convolution_convert_fusion = bf16[7168,3584]{1,0:T(8,128)(2,1)} fusion(bf16[256,7168]{1,0:T(8,128)(2,1)} %all-gather.9.cloned.1.call-done, bf16[256,3584]{1,0:T(8,128)(2,1)} %all-gather.11.cloned.1.call-done), kind=kOutput, calls=%fused_computation | convolution fusion | flops 13179027456 | bytes 56885248 | tf_op jit(solution)/shard_map/dot_general | solution.py:50
  740.0 0.0 reduce-scatter.5.cloned.1.call-update
  740.1 837.7 %reduce-scatter.5.cloned.1.call-done = bf16[1792,3584]{1,0:T(8,128)(2,1)} async-done(((bf16[7168,3584]{1,0:T(8,128)(2,1)}), bf16[1792,3584]{1,0:T(8,128)(2,1)}) %reduce-scatter.5.cloned.1.call-update) | async-done | bytes 12845072 | tf_op jit(solution)/shard_map/reduce_scatter | solution.py:49
  1577.7 14.1 convert_multiply_fusion
  (5 shorter events, 0.0 us)
Async XLA Ops:
  6.5 42.2 %all-gather.5.cloned.1.call-start = ((), (), s32[]{:S(2)}) async-start(), calls=%async_computation.2 | async-start | bytes 4718592 | tf_op jit(solution)/shard_map/all_gather | solution.py:13
  7.3 80.1 %all-gather.7.cloned.1.call-start = ((), (), s32[]{:S(2)}) async-start(), calls=%async_computation.3 | async-start | bytes 4718592 | tf_op jit(solution)/shard_map/all_gather | solution.py:14
  7.3 17.9 %slice-start = ((s8[14680064]{0:T(1024)(128)(4,1)}), s8[2097152]{0:T(1024)(128)(4,1)S(1)}, s32[]{:S(2)}) async-start(s8[14680064]{0:T(1024)(128)(4,1)} %bitcast.11), calls=%async_computation.8 | async-start | bytes 4194304
  8.0 602.7 %reduce-scatter.3.cloned.1.call-start = ((), (), s32[]{:S(2)}) async-start(), calls=%async_computation.4 | async-start | bytes 36700160 | tf_op jit(solution)/shard_map/reduce_scatter | solution.py:26
  8.1 17.1 %slice-start.1 = ((s8[14680064]{0:T(1024)(128)(4,1)}), s8[4194304]{0:T(1024)(128)(4,1)S(1)}, s32[]{:S(2)}) async-start(s8[14680064]{0:T(1024)(128)(4,1)} %bitcast.11), calls=%async_computation.9 | async-start | bytes 8388608
  8.1 17.1 %slice-start.2 = ((s8[14680064]{0:T(1024)(128)(4,1)}), s8[4194304]{0:T(1024)(128)(4,1)S(1)}, s32[]{:S(2)}) async-start(s8[14680064]{0:T(1024)(128)(4,1)} %bitcast.11), calls=%async_computation.10 | async-start | bytes 8388608
  8.1 17.1 %slice-start.3 = ((s8[14680064]{0:T(1024)(128)(4,1)}), s8[4194304]{0:T(1024)(128)(4,1)S(1)}, s32[]{:S(2)}) async-start(s8[14680064]{0:T(1024)(128)(4,1)} %bitcast.11), calls=%async_computation.11 | async-start | bytes 8388608
  87.3 23.2 %copy-start = (f32[1024,3584]{1,0:T(8,128)S(1)}, f32[1024,3584]{1,0:T(8,128)}, u32[]{:S(2)}) copy-start(f32[1024,3584]{1,0:T(8,128)} %fusion.2) | copy-start | bytes 44040196
  128.9 555.8 %all-gather.11.cloned.1.call-start = ((), (), s32[]{:S(2)}) async-start(), calls=%async_computation.6 | async-start | bytes 2752512 | tf_op jit(solution)/shard_map/all_gather | solution.py:48
  655.8 62.0 %all-gather.9.cloned.1.call-start = ((), (), s32[]{:S(2)}) async-start(), calls=%async_computation.5 | async-start | bytes 4587520 | tf_op jit(solution)/shard_map/all_gather | solution.py:47
  656.9 920.8 %reduce-scatter.5.cloned.1.call-start = ((), (), s32[]{:S(2)}) async-start(), calls=%async_computation.7 | async-start | bytes 64225280 | tf_op jit(solution)/shard_map/reduce_scatter | solution.py:49
Sparse Core Ops, SparseCore 0:
  9.2 39.4 all-gather.4
  50.6 36.7 all-gather.6
  129.0 481.6 reduce-scatter.2
  655.9 28.8 all-gather.10
  686.2 31.4 all-gather.8
  740.2 837.5 reduce-scatter.4
where the time goes:
time: 1600 us
  waiting for transfers between devices  1410 us (88%)
  matrix products  68.2 us (4%)
  other arithmetic  43.5 us (3%)
  blocking collectives  35.2 us (2%)
  local copies, waits for them, and re-layouts  24.3 us (2%)
    reduce_scatter x1, waiting for transfers between devices, local(): lax.psum_scatter(lax.dot_general(block_first, block_second, (((0,), (0,))...  838 us
    reduce_scatter x1, waiting for transfers between devices, local(): lax.psum_scatter(jnp.concatenate([term_first, term_second], axis=1), 'tok...  482 us
    all_gather x1, waiting for transfers between devices, local(): block_first = lax.all_gather(norm_first, 'col', axis=1, tiled=True)  33 us
  transfers between devices with their start and end apart: 6, of which 6 were waited for; matrix products, arithmetic and copies ran while one was open for 3% of the time, Pallas kernels for 0%

commit v1 on v0

v1 whole, which is shorter than its diff:
```python
import jax
import jax.numpy as jnp
from jax import lax
from jax.sharding import PartitionSpec as P

HALVES = 2
PIECES = 2
CARRY = jnp.float16


def reduce_to_owner(part, depth):
    me = lax.axis_index("tok")

    def own(d):
        d = jnp.clip(d, 0, depth - 1)
        return lax.dynamic_index_in_dim(part, d, axis=1, keepdims=False).astype(jnp.float32)

    up = down = None
    for step in range(1, depth):
        rise = own(depth - step + me)
        fall = own(step - depth + me)
        if up is not None:
            rise = rise + up.astype(jnp.float32)
            fall = fall + down.astype(jnp.float32)
        up = lax.ppermute(rise.astype(CARRY), "tok", [(i, i + 1) for i in range(step)])
        down = lax.ppermute(
            fall.astype(CARRY), "tok", [(depth - 1 - i, depth - 2 - i) for i in range(step)]
        )
    return own(me) + up.astype(jnp.float32) + down.astype(jnp.float32)


def normalize(summed):
    gate, upward = summed[0], summed[1]
    act = jax.nn.silu(gate) * upward
    inverse = 1.0 / act.shape[1]
    dev = act - jnp.sum(act, axis=1, keepdims=True) * inverse
    spread = jnp.sum(dev * dev, axis=1, keepdims=True) * inverse
    return (dev * lax.rsqrt(spread + 1e-05)).astype(jnp.bfloat16)


def owned_norms(full, weights, half, depth):
    size = weights.shape[2] // HALVES
    part = lax.dot_general(
        weights[:, :, half * size : (half + 1) * size],
        full,
        (((0,), (1,)), ((), ())),
        preferred_element_type=jnp.float32,
    ).astype(CARRY)
    width = size // (depth * PIECES)
    part = part.reshape(2, depth, PIECES, width, full.shape[0])
    return jnp.concatenate(
        [normalize(reduce_to_owner(part[:, :, q], depth)) for q in range(PIECES)], axis=0
    )


def local(first_inputs, second_inputs, first_weights, second_weights):
    depth = lax.axis_size("tok")
    wide = lax.axis_size("col")
    rows = lax.axis_size("row")
    full_second = lax.all_gather(second_inputs, ("row", "col"), axis=0, tiled=True)
    full_first = lax.all_gather(first_inputs, ("row", "col"), axis=0, tiled=True)
    tokens = full_first.shape[0]
    second = []
    for half in range(HALVES):
        norm = owned_norms(full_second, second_weights, half, depth)
        norm = lax.all_gather(norm, ("row", "tok"), axis=0, tiled=True)
        second.append(norm.reshape(rows, -1, tokens))
    second = jnp.concatenate(second, axis=1).reshape(-1, tokens)
    first = []
    for half in range(HALVES):
        norm = owned_norms(full_first, first_weights, half, depth)
        if wide == depth:
            swap = [(c * depth + t, t * depth + c) for c in range(wide) for t in range(depth)]
            norm = lax.ppermute(norm, ("col", "tok"), swap)
            norm = lax.all_gather(norm, "col", axis=0, tiled=True)
        else:
            norm = lax.all_gather(norm, ("col", "tok"), axis=0, tiled=True)
            norm = norm.reshape(wide, -1, tokens)
        first.append(norm)
    if wide == depth:
        first = jnp.concatenate(first, axis=0)
    else:
        first = jnp.concatenate(first, axis=1).reshape(-1, tokens)
        count = first.shape[0] // depth
        first = lax.dynamic_slice_in_dim(first, lax.axis_index("tok") * count, count, axis=0)
    total = lax.dot_general(
        first, second, (((1,), (1,)), ((), ())), preferred_element_type=jnp.float32
    )
    return total * float(tokens) ** (-0.5)


def solution(mesh):
    placed = (
        P(("row", "col"), "tok"),
        P(("row", "col"), "tok"),
        P("tok", None, ("row", "col")),
        P("tok", None, ("col", "row")),
    )
    return jax.shard_map(
        local, mesh=mesh, in_specs=placed, out_specs=P(("row", "tok"), "col"), check_vma=False
    )
```

time: 1600 us -> 550 us (0.34)
  waiting for transfers between devices: 1410 us -> 251 us
  starting transfers between devices: 0.2 us -> 129 us
  blocking collectives: 35.2 us -> 0 us
  local copies, waits for them, and re-layouts: 24.3 us -> 43.6 us
    reduce_scatter x2 -> x0, waiting for transfers between devices: 1320 us -> none  [the longest x1 838 us: local(): lax.psum_scatter(lax.dot_general(block_first, block_second, (((0,), (0,))...]
    ppermute x0 -> x50, waiting for transfers between devices: none -> 163 us  [the longest x24 109 us: reduce_to_owner(): lax.ppermute(rise.astype(CARRY), 'tok', [(i, i + 1) for i in range(step)])]
    ppermute x0 -> x50, starting transfers between devices: none -> 129 us  [the longest x24 106 us: reduce_to_owner(): lax.ppermute(rise.astype(CARRY), 'tok', [(i, i + 1) for i in range(step)])]
    psum x2 -> x0, blocking collectives: 35.2 us -> none  [the longest x1 19.6 us: local(): lax.psum((jnp.sum(act_first, axis=0), jnp.sum(act_second, axis=0)), 'tok')]
    slice x0 -> x6, local copies, waits for them, and re-layouts: none -> 33.4 us  [the longest x2 24.4 us: owned_norms(): weights[:, :, half * size:(half + 1) * size]]
    unnamed x12 -> x36, local copies, waits for them, and re-layouts: 24.3 us -> 4.12 us
    all_gather x1, waiting for transfers between devices: 16.3 us -> 0.02 us  [local(): lax.all_gather(first_inputs, ('row', 'col'), axis=0, tiled=True)]
    all_gather x2 -> x4, waiting for transfers between devices: 60.8 us -> 58.4 us  [the longest x2 58.3 us: local(): norm = lax.all_gather(norm, 'col', axis=0, tiled=True)]
  transfers between devices with their start and end apart: 6 -> 56, of which waited for: 6 -> 20; matrix products, arithmetic and copies ran while one was open for 3% -> 22% of each run, Pallas kernels for 0% -> 0%
where the time goes in v1:
time: 550 us; the launch traced here: 542 us
  waiting for transfers between devices  251 us (46%)
  starting transfers between devices  129 us (23%)
  matrix products  70 us (13%)
  local copies, waits for them, and re-layouts  43.6 us (8%)
  other arithmetic  32.8 us (6%)
  between operations  15.1 us (3%)
    ppermute x24, waiting for transfers between devices, reduce_to_owner(): lax.ppermute(rise.astype(CARRY), 'tok', [(i, i + 1) for i in range(step)])  109 us
    ppermute x24, starting transfers between devices, reduce_to_owner(): lax.ppermute(rise.astype(CARRY), 'tok', [(i, i + 1) for i in range(step)])  106 us
    all_gather x2, waiting for transfers between devices, local(): norm = lax.all_gather(norm, 'col', axis=0, tiled=True)  58.3 us
    ppermute x24, waiting for transfers between devices, reduce_to_owner(): lax.ppermute(fall.astype(CARRY), 'tok', [(depth - 1 - i, depth - 2 - i) f...  54.8 us
    dot_general x4, matrix products, owned_norms(): lax.dot_general(weights[:, :, half * size:(half + 1) * size], full, (((0,...  48.2 us
    all_gather x1, waiting for transfers between devices, local(): lax.all_gather(second_inputs, ('row', 'col'), axis=0, tiled=True)  27.8 us
    slice x2, local copies, waits for them, and re-layouts, owned_norms(): weights[:, :, half * size:(half + 1) * size]  24.4 us
    dot_general x1, matrix products, local(): lax.dot_general(first, second, (((1,), (1,)), ((), ())), preferred_elemen...  21.8 us
  transfers between devices with their start and end apart: 56, of which 20 were waited for; matrix products, arithmetic and copies ran while one was open for 22% of the time, Pallas kernels for 0%

profile of v1, /device:TPU:0, one launch (start us, length us, event | category | flops | bytes accessed | tf_op | source)
XLA Modules:
  0.0 541.8 jit_solution(11249596553578190079)
XLA Ops:
  8.1 12.8 %fusion.101 = (bf16[2048,2,896]{2,1,0:T(2,128)(2,1)}, bf16[2048,2,896]{2,1,0:T(2,128)(2,1)}) fusion(bf16[2048,2,1792]{2,1,0:T(2,128)(2,1)} %param.7), kind=kLoop, calls=%fused_computation.187 | loop fusion | bytes 29360128 | tf_op jit(solution)/shard_map/slice | solution.py:44
  20.8 27.8 %all-gather.13.cloned.1.call-done = bf16[1024,2048]{1,0:T(8,128)(2,1)} async-done(((bf16[128,2048]{1,0:T(8,128)(2,1)}), bf16[1024,2048]{1,0:T(8,128)(2,1)}) %all-gather.13.cloned.1.call-update) | async-done | bytes 4194320 | tf_op jit(solution)/shard_map/all_gather | solution.py:60
  48.7 12.0 %fusion.30 = f16[2,896,1024]{2,1,0:T(8,128)(2,1)S(1)} fusion(bf16[1024,2048]{1,0:T(8,128)(2,1)} %all-gather.13.cloned.1.call-done, bf16[2048,2,896]{2,1,0:T(2,128)(2,1)} %get-tuple-element.24), kind=kOutput, calls=%fused_computation.20 | convolution fusion | flops 7518027776 | bytes 15204352 | tf_op jit(solution)/shard_map/dot_general | solution.py:43
  63.9 4.2 collective-permute-start.38
  68.2 2.1 collective-permute-start.44
  70.3 11.6 %fusion.100 = (bf16[2048,2,896]{2,1,0:T(2,128)(2,1)}, bf16[2048,2,896]{2,1,0:T(2,128)(2,1)}) fusion(bf16[2048,2,1792]{2,1,0:T(2,128)(2,1)S(1)} %bitcast.365), kind=kLoop, calls=%fused_computation.186 | loop fusion | bytes 29360128 | tf_op jit(solution)/shard_map/slice | solution.py:44
  83.4 1.4 fusion.42
  84.8 1.3 collective-permute-start.39
  86.1 2.1 collective-permute-done.44
  89.4 5.0 collective-permute-start.45
  94.4 11.9 %fusion.25 = f16[2,896,1024]{2,1,0:T(8,128)(2,1)S(1)} fusion(bf16[1024,2048]{1,0:T(8,128)(2,1)} %all-gather.13.cloned.1.call-done, bf16[2048,2,896]{2,1,0:T(2,128)(2,1)} %get-tuple-element.23), kind=kOutput, calls=%fused_computation.19 | convolution fusion | flops 7518027776 | bytes 15204352 | tf_op jit(solution)/shard_map/dot_general | solution.py:43
  112.4 5.4 collective-permute-start.26
  117.8 2.0 collective-permute-start.40
  119.8 3.2 collective-permute-start.46
  125.3 2.0 fusion.36
  128.6 13.1 %fusion.20 = f16[2,896,1024]{2,1,0:T(8,128)(2,1)} fusion(bf16[1024,2048]{1,0:T(8,128)(2,1)} %all-gather.7.cloned.1.call-done, bf16[2048,2,896]{2,1,0:T(2,128)(2,1)} %get-tuple-element.22), kind=kOutput, calls=%fused_computation.18 | convolution fusion | flops 7518027776 | bytes 15204352 | tf_op jit(solution)/shard_map/dot_general | solution.py:43
  143.5 9.9 %collective-permute-start.32 = (f16[2,112,1024]{2,1,0:T(8,128)(2,1)}, f16[2,112,1024]{2,1,0:T(8,128)(2,1)}, u32[]{:S(2)}, u32[]{:S(2)}) collective-permute-start(f16[2,112,1024]{2,1,0:T(8,128)(2,1)} %get-tuple-element.55), channel_id=1, source_target_pairs={{0,1},{4,5},{8,9},{12,13},{16,17},{20,21},{24,25},{28,29}} | collective-permute-start | bytes 1376264 | tf_op jit(solution)/shard_map/ppermute | solution.py:25
  153.4 1.6 fusion.44
  155.7 1.4 fusion.39
  159.1 1.3 fusion.52
  160.5 1.3 collective-permute-start.27
  163.0 4.5 collective-permute-start.33
  167.5 3.5 fusion.103
  172.1 3.2 collective-permute-start.13
  175.3 1.7 collective-permute-done.27
  178.1 18.5 %collective-permute-done.33 = f16[2,112,1024]{2,1,0:T(8,128)(2,1)S(1)} collective-permute-done((f16[2,112,1024]{2,1,0:T(8,128)(2,1)S(1)}, f16[2,112,1024]{2,1,0:T(8,128)(2,1)S(1)}, u32[]{:S(2)}, u32[]{:S(2)}) %collective-permute-start.33) | collective-permute-done | bytes 458784 | tf_op jit(solution)/shard_map/ppermute | solution.py:25
  197.8 11.2 %fusion.15 = f16[2,896,1024]{2,1,0:T(8,128)(2,1)S(1)} fusion(bf16[1024,2048]{1,0:T(8,128)(2,1)S(1)} %copy-done.13, bf16[2048,2,896]{2,1,0:T(2,128)(2,1)} %get-tuple-element.21), kind=kOutput, calls=%fused_computation.17 | convolution fusion | flops 7518027776 | bytes 15204352 | tf_op jit(solution)/shard_map/dot_general | solution.py:43
  209.0 5.0 collective-permute-start.28
  214.0 4.5 collective-permute-start.34
  218.8 1.3 collective-permute-start.31
  220.3 1.3 collective-permute-start.37
  221.6 3.2 fusion.102
  224.8 9.0 %collective-permute-done.28 = f16[2,112,1024]{2,1,0:T(8,128)(2,1)S(1)} collective-permute-done((f16[2,112,1024]{2,1,0:T(8,128)(2,1)S(1)}, f16[2,112,1024]{2,1,0:T(8,128)(2,1)S(1)}, u32[]{:S(2)}, u32[]{:S(2)}) %collective-permute-start.28) | collective-permute-done | bytes 458784 | tf_op jit(solution)/shard_map/ppermute | solution.py:25
  234.7 14.8 %collective-permute-done.31 = f16[2,112,1024]{2,1,0:T(8,128)(2,1)S(1)} collective-permute-done((f16[2,112,1024]{2,1,0:T(8,128)(2,1)S(1)}, f16[2,112,1024]{2,1,0:T(8,128)(2,1)S(1)}, u32[]{:S(2)}, u32[]{:S(2)}) %collective-permute-start.31) | collective-permute-done | bytes 458784 | tf_op jit(solution)/shard_map/ppermute | solution.py:26
  249.7 5.2 collective-permute-done.37
  257.4 5.8 %collective-permute-start.19 = (f16[2,112,1024]{2,1,0:T(8,128)(2,1)S(1)}, f16[2,112,1024]{2,1,0:T(8,128)(2,1)S(1)}, u32[]{:S(2)}, u32[]{:S(2)}) collective-permute-start(f16[2,112,1024]{2,1,0:T(8,128)(2,1)S(1)} %get-tuple-element.47), channel_id=1, source_target_pairs={{0,1},{4,5},{8,9},{12,13},{16,17},{20,21},{24,25},{28,29}} | collective-permute-start | bytes 1376264 | tf_op jit(solution)/shard_map/ppermute | solution.py:25
  263.9 1.3 dynamic-slice_bitcast_fusion.15
  265.2 1.3 collective-permute-start
  268.6 8.9 %collective-permute-done.19 = f16[2,112,1024]{2,1,0:T(8,128)(2,1)S(1)} collective-permute-done((f16[2,112,1024]{2,1,0:T(8,128)(2,1)S(1)}, f16[2,112,1024]{2,1,0:T(8,128)(2,1)S(1)}, u32[]{:S(2)}, u32[]{:S(2)}) %collective-permute-start.19) | collective-permute-done | bytes 458784 | tf_op jit(solution)/shard_map/ppermute | solution.py:25
  277.5 4.4 collective-permute-start.6
  282.1 15.1 %collective-permute-done = f16[2,112,1024]{2,1,0:T(8,128)(2,1)S(1)} collective-permute-done((f16[2,112,1024]{2,1,0:T(8,128)(2,1)S(1)}, f16[2,112,1024]{2,1,0:T(8,128)(2,1)S(1)}, u32[]{:S(2)}, u32[]{:S(2)}) %collective-permute-start) | collective-permute-done | bytes 458784 | tf_op jit(solution)/shard_map/ppermute | solution.py:25
  297.2 4.4 collective-permute-start.14
  301.8 7.8 %collective-permute-done.6 = f16[2,112,1024]{2,1,0:T(8,128)(2,1)S(1)} collective-permute-done((f16[2,112,1024]{2,1,0:T(8,128)(2,1)S(1)}, f16[2,112,1024]{2,1,0:T(8,128)(2,1)S(1)}, u32[]{:S(2)}, u32[]{:S(2)}) %collective-permute-start.6) | collective-permute-done | bytes 458784 | tf_op jit(solution)/shard_map/ppermute | solution.py:25
  309.6 4.4 collective-permute-start.20
  314.9 14.4 %collective-permute-done.14 = f16[2,112,1024]{2,1,0:T(8,128)(2,1)S(1)} collective-permute-done((f16[2,112,1024]{2,1,0:T(8,128)(2,1)S(1)}, f16[2,112,1024]{2,1,0:T(8,128)(2,1)S(1)}, u32[]{:S(2)}, u32[]{:S(2)}) %collective-permute-start.14) | collective-permute-done | bytes 458784 | tf_op jit(solution)/shard_map/ppermute | solution.py:25
  329.2 4.4 collective-permute-start.1
  334.1 1.9 collective-permute-start.7
  336.0 12.9 %collective-permute-done.20 = f16[2,112,1024]{2,1,0:T(8,128)(2,1)S(1)} collective-permute-done((f16[2,112,1024]{2,1,0:T(8,128)(2,1)S(1)}, f16[2,112,1024]{2,1,0:T(8,128)(2,1)S(1)}, u32[]{:S(2)}, u32[]{:S(2)}) %collective-permute-start.20) | collective-permute-done | bytes 458784 | tf_op jit(solution)/shard_map/ppermute | solution.py:25
  348.9 4.4 collective-permute-start.15
  354.4 13.0 %collective-permute-done.1 = f16[2,112,1024]{2,1,0:T(8,128)(2,1)S(1)} collective-permute-done((f16[2,112,1024]{2,1,0:T(8,128)(2,1)S(1)}, f16[2,112,1024]{2,1,0:T(8,128)(2,1)S(1)}, u32[]{:S(2)}, u32[]{:S(2)}) %collective-permute-start.1) | collective-permute-done | bytes 458784 | tf_op jit(solution)/shard_map/ppermute | solution.py:25
  367.5 4.4 collective-permute-start.21
  373.1 4.3 collective-permute-done.7
  377.3 4.4 collective-permute-start.2
  383.1 1.3 collective-permute-start.18
  384.6 1.3 collective-permute-start.24
  387.2 14.4 %collective-permute-start.8 = (f16[2,112,1024]{2,1,0:T(8,128)(2,1)S(1)}, f16[2,112,1024]{2,1,0:T(8,128)(2,1)S(1)}, u32[]{:S(2)}, u32[]{:S(2)}) collective-permute-start(f16[2,112,1024]{2,1,0:T(8,128)(2,1)S(1)} %get-tuple-element.37), channel_id=1, source_target_pairs={{0,1},{1,2},{2,3},{4,5},{5,6},{6,7},{8,9},{9,10},{10,11},{12,13},{... | collective-permute-start | bytes 1376264 | tf_op jit(solution)/shard_map/ppermute | solution.py:25
  402.6 1.3 collective-permute-start.5
  403.9 6.5 %collective-permute-done.24 = f16[2,112,1024]{2,1,0:T(8,128)(2,1)S(1)} collective-permute-done((f16[2,112,1024]{2,1,0:T(8,128)(2,1)S(1)}, f16[2,112,1024]{2,1,0:T(8,128)(2,1)S(1)}, u32[]{:S(2)}, u32[]{:S(2)}) %collective-permute-start.24) | collective-permute-done | bytes 458784 | tf_op jit(solution)/shard_map/ppermute | solution.py:26
  413.9 3.4 collective-permute-done.5
  418.4 24.9 %collective-permute-done.11 = f16[2,112,1024]{2,1,0:T(8,128)(2,1)S(1)} collective-permute-done((f16[2,112,1024]{2,1,0:T(8,128)(2,1)S(1)}, f16[2,112,1024]{2,1,0:T(8,128)(2,1)S(1)}, u32[]{:S(2)}, u32[]{:S(2)}) %collective-permute-start.11) | collective-permute-done | bytes 458784 | tf_op jit(solution)/shard_map/ppermute | solution.py:26
  447.5 6.9 %pad_maximum_fusion = bf16[2,1792,1024]{2,1,0:T(8,128)(2,1)} fusion(bf16[2,896,1024]{2,1,0:T(8,128)(2,1)} %bitcast.367, bf16[2,896,1024]{2,1,0:T(8,128)(2,1)} %bitcast.368), kind=kLoop, calls=%fused_computation.1 | loop fusion | flops 14680064 | bytes 14680064 | tf_op jit(solution)/shard_map/concatenate | solution.py:68
  454.4 31.8 %all-gather.11.cloned.1.call-done = bf16[896,1024]{1,0:T(8,128)(2,1)} async-done(((bf16[224,1024]{1,0:T(8,128)(2,1)}), bf16[896,1024]{1,0:T(8,128)(2,1)}) %all-gather.11.cloned.1.call-update) | async-done | bytes 1835024 | tf_op jit(solution)/shard_map/all_gather | solution.py:75
  486.2 26.5 %all-gather.9.cloned.1.call-done = bf16[896,1024]{1,0:T(8,128)(2,1)} async-done(((bf16[224,1024]{1,0:T(8,128)(2,1)}), bf16[896,1024]{1,0:T(8,128)(2,1)}) %all-gather.9.cloned.1.call-update) | async-done | bytes 1835024 | tf_op jit(solution)/shard_map/all_gather | solution.py:75
  512.7 21.8 %convolution_multiply_fusion = f32[1792,3584]{1,0:T(8,128)} fusion(bf16[3584,1024]{1,0:T(8,128)(2,1)} %bitcast.366, bf16[896,1024]{1,0:T(8,128)(2,1)} %all-gather.11.cloned.1.call-done, bf16[896,1024]{1,0:T(8,128)(2,1)} %all-gather.9.cloned.1.call-done), kind=kOutput, calls=%fused_computation | convolution fusion | flops 13167099904 | bytes 36700160 | tf_op jit(solution)/shard_map/dot_general | solution.py:86
  (183 shorter events, 48.8 us)
Async XLA Ops:
  6.5 42.2 %all-gather.13.cloned.1.call-start = ((), (), s32[]{:S(2)}) async-start(), calls=%async_computation.3 | async-start | bytes 4718592 | tf_op jit(solution)/shard_map/all_gather | solution.py:60
  7.3 121.3 %all-gather.7.cloned.1.call-start = ((), (), s32[]{:S(2)}) async-start(), calls=%async_computation | async-start | bytes 4718592 | tf_op jit(solution)/shard_map/all_gather | solution.py:61
  8.0 439.5 %all-gather.17.cloned.1.call-start = ((), (), s32[]{:S(2)}) async-start(), calls=%async_computation.5 | async-start | bytes 4128768 | tf_op jit(solution)/shard_map/all_gather | solution.py:66
  48.7 21.6 %slice-start.2 = ((s8[14680064]{0:T(1024)(128)(4,1)}), s8[4194304]{0:T(1024)(128)(4,1)S(1)}, s32[]{:S(2)}) async-start(s8[14680064]{0:T(1024)(128)(4,1)} %bitcast.364), calls=%async_computation.8 | async-start | bytes 8388608
  48.7 21.6 %slice-start.3 = ((s8[14680064]{0:T(1024)(128)(4,1)}), s8[2097152]{0:T(1024)(128)(4,1)S(1)}, s32[]{:S(2)}) async-start(s8[14680064]{0:T(1024)(128)(4,1)} %bitcast.364), calls=%async_computation.9 | async-start | bytes 4194304
  61.7 45.8 %copy-start.7 = (f16[2,4,1,112,1024]{4,3,2,1,0:T(8,128)(2,1)}, f16[2,4,1,112,1024]{4,3,2,1,0:T(8,128)(2,1)S(1)}, u32[]{:S(2)}) copy-start(f16[2,4,1,112,1024]{4,3,2,1,0:T(8,128)(2,1)S(1)} %get-tuple-element.32) | copy-start | bytes 5505028
  63.9 19.5 %collective-permute-start.38 = (f16[2,112,1024]{2,1,0:T(8,128)(2,1)}, f16[2,112,1024]{2,1,0:T(8,128)(2,1)}, u32[]{:S(2)}, u32[]{:S(2)}) collective-permute-start(f16[2,112,1024]{2,1,0:T(8,128)(2,1)} %get-tuple-element.59), channel_id=1, source_target_pairs={{0,1},{4,5},{8,9},{12,13},{16,17},{20,21},{24,25},{28,29}} | collective-permute-start | bytes 1376264 | tf_op jit(solution)/shard_map/ppermute | solution.py:25
  68.2 19.9 %collective-permute-start.44 = (f16[2,112,1024]{2,1,0:T(8,128)(2,1)S(1)}, f16[2,112,1024]{2,1,0:T(8,128)(2,1)}, u32[]{:S(2)}, u32[]{:S(2)}) collective-permute-start(f16[2,112,1024]{2,1,0:T(8,128)(2,1)S(1)} %get-tuple-element.63), channel_id=1, source_target_pairs={{0,1},{4,5},{8,9},{12,13},{16,17},{20,21},{24,25},{28,29}} | collective-permute-start | bytes 1376264 | tf_op jit(solution)/shard_map/ppermute | solution.py:25
  82.0 24.4 %collective-permute-start.41 = (f16[2,112,1024]{2,1,0:T(8,128)(2,1)S(1)}, f16[2,112,1024]{2,1,0:T(8,128)(2,1)S(1)}, u32[]{:S(2)}, u32[]{:S(2)}) collective-permute-start(f16[2,112,1024]{2,1,0:T(8,128)(2,1)S(1)} %get-tuple-element.60), channel_id=1, source_target_pairs={{3,2},{7,6},{11,10},{15,14},{19,18},{23,22},{27,26},{31,30}} | collective-permute-start | bytes 1376264 | tf_op jit(solution)/shard_map/ppermute | solution.py:26
  82.7 24.9 %collective-permute-start.47 = (f16[2,112,1024]{2,1,0:T(8,128)(2,1)S(1)}, f16[2,112,1024]{2,1,0:T(8,128)(2,1)S(1)}, u32[]{:S(2)}, u32[]{:S(2)}) collective-permute-start(f16[2,112,1024]{2,1,0:T(8,128)(2,1)S(1)} %get-tuple-element.64), channel_id=1, source_target_pairs={{3,2},{7,6},{11,10},{15,14},{19,18},{23,22},{27,26},{31,30}} | collective-permute-start | bytes 1376264 | tf_op jit(solution)/shard_map/ppermute | solution.py:26
  84.8 21.6 %collective-permute-start.39 = (f16[2,112,1024]{2,1,0:T(8,128)(2,1)S(1)}, f16[2,112,1024]{2,1,0:T(8,128)(2,1)S(1)}, u32[]{:S(2)}, u32[]{:S(2)}) collective-permute-start(f16[2,112,1024]{2,1,0:T(8,128)(2,1)S(1)} %fusion.42), channel_id=1, source_target_pairs={{0,1},{1,2},{4,5},{5,6},{8,9},{9,10},{12,13},{13,14},{16,17},{17,1... | collective-permute-start | bytes 1376264 | tf_op jit(solution)/shard_map/ppermute | solution.py:25
  89.4 18.2 %collective-permute-start.45 = (f16[2,112,1024]{2,1,0:T(8,128)(2,1)S(1)}, f16[2,112,1024]{2,1,0:T(8,128)(2,1)S(1)}, u32[]{:S(2)}, u32[]{:S(2)}) collective-permute-start(f16[2,112,1024]{2,1,0:T(8,128)(2,1)S(1)} %fusion.37), channel_id=1, source_target_pairs={{0,1},{1,2},{4,5},{5,6},{8,9},{9,10},{12,13},{13,14},{16,17},{17,1... | collective-permute-start | bytes 1376264 | tf_op jit(solution)/shard_map/ppermute | solution.py:25
  106.8 16.2 %collective-permute-start.42 = (f16[2,112,1024]{2,1,0:T(8,128)(2,1)S(1)}, f16[2,112,1024]{2,1,0:T(8,128)(2,1)S(1)}, u32[]{:S(2)}, u32[]{:S(2)}) collective-permute-start(f16[2,112,1024]{2,1,0:T(8,128)(2,1)S(1)} %get-tuple-element.58), channel_id=1, source_target_pairs={{3,2},{2,1},{7,6},{6,5},{11,10},{10,9},{15,14},{14,13},{19,18},{18... | collective-permute-start | bytes 1376264 | tf_op jit(solution)/shard_map/ppermute | solution.py:26
  108.0 17.3 %collective-permute-start.48 = (f16[2,112,1024]{2,1,0:T(8,128)(2,1)S(1)}, f16[2,112,1024]{2,1,0:T(8,128)(2,1)S(1)}, u32[]{:S(2)}, u32[]{:S(2)}) collective-permute-start(f16[2,112,1024]{2,1,0:T(8,128)(2,1)S(1)} %get-tuple-element.62), channel_id=1, source_target_pairs={{3,2},{2,1},{7,6},{6,5},{11,10},{10,9},{15,14},{14,13},{19,18},{18... | collective-permute-start | bytes 1376264 | tf_op jit(solution)/shard_map/ppermute | solution.py:26
  110.0 51.9 %copy-start.3 = (f16[2,4,1,112,1024]{4,3,2,1,0:T(8,128)(2,1)}, f16[2,4,1,112,1024]{4,3,2,1,0:T(8,128)(2,1)S(1)}, u32[]{:S(2)}) copy-start(f16[2,4,1,112,1024]{4,3,2,1,0:T(8,128)(2,1)S(1)} %get-tuple-element.30) | copy-start | bytes 5505028
  112.4 46.7 %collective-permute-start.26 = (f16[2,112,1024]{2,1,0:T(8,128)(2,1)}, f16[2,112,1024]{2,1,0:T(8,128)(2,1)}, u32[]{:S(2)}, u32[]{:S(2)}) collective-permute-start(f16[2,112,1024]{2,1,0:T(8,128)(2,1)} %get-tuple-element.51), channel_id=1, source_target_pairs={{0,1},{4,5},{8,9},{12,13},{16,17},{20,21},{24,25},{28,29}} | collective-permute-start | bytes 1376264 | tf_op jit(solution)/shard_map/ppermute | solution.py:25
  117.8 25.0 %collective-permute-start.40 = (f16[2,112,1024]{2,1,0:T(8,128)(2,1)S(1)}, f16[2,112,1024]{2,1,0:T(8,128)(2,1)}, u32[]{:S(2)}, u32[]{:S(2)}) collective-permute-start(f16[2,112,1024]{2,1,0:T(8,128)(2,1)S(1)} %get-tuple-element.57), channel_id=1, source_target_pairs={{0,1},{1,2},{2,3},{4,5},{5,6},{6,7},{8,9},{9,10},{10,11},{12,13},{... | collective-permute-start | bytes 1376264 | tf_op jit(solution)/shard_map/ppermute | solution.py:25
  119.8 35.2 %collective-permute-start.46 = (f16[2,112,1024]{2,1,0:T(8,128)(2,1)S(1)}, f16[2,112,1024]{2,1,0:T(8,128)(2,1)S(1)}, u32[]{:S(2)}, u32[]{:S(2)}) collective-permute-start(f16[2,112,1024]{2,1,0:T(8,128)(2,1)S(1)} %get-tuple-element.61), channel_id=1, source_target_pairs={{0,1},{1,2},{2,3},{4,5},{5,6},{6,7},{8,9},{9,10},{10,11},{12,13},{... | collective-permute-start | bytes 1376264 | tf_op jit(solution)/shard_map/ppermute | solution.py:25
  124.0 19.5 %collective-permute-start.43 = (f16[2,112,1024]{2,1,0:T(8,128)(2,1)}, f16[2,112,1024]{2,1,0:T(8,128)(2,1)}, u32[]{:S(2)}, u32[]{:S(2)}) collective-permute-start(f16[2,112,1024]{2,1,0:T(8,128)(2,1)} %fusion.41), channel_id=1, source_target_pairs={{3,2},{2,1},{1,0},{7,6},{6,5},{5,4},{11,10},{10,9},{9,8},{15,14},{... | collective-permute-start | bytes 1376264 | tf_op jit(solution)/shard_map/ppermute | solution.py:26
  127.3 28.4 %collective-permute-start.49 = (f16[2,112,1024]{2,1,0:T(8,128)(2,1)}, f16[2,112,1024]{2,1,0:T(8,128)(2,1)}, u32[]{:S(2)}, u32[]{:S(2)}) collective-permute-start(f16[2,112,1024]{2,1,0:T(8,128)(2,1)} %fusion.36), channel_id=1, source_target_pairs={{3,2},{2,1},{1,0},{7,6},{6,5},{5,4},{11,10},{10,9},{9,8},{15,14},{... | collective-permute-start | bytes 1376264 | tf_op jit(solution)/shard_map/ppermute | solution.py:26
  142.8 32.5 %collective-permute-start.29 = (f16[2,112,1024]{2,1,0:T(8,128)(2,1)}, f16[2,112,1024]{2,1,0:T(8,128)(2,1)S(1)}, u32[]{:S(2)}, u32[]{:S(2)}) collective-permute-start(f16[2,112,1024]{2,1,0:T(8,128)(2,1)} %get-tuple-element.52), channel_id=1, source_target_pairs={{3,2},{7,6},{11,10},{15,14},{19,18},{23,22},{27,26},{31,30}} | collective-permute-start | bytes 1376264 | tf_op jit(solution)/shard_map/ppermute | solution.py:26
  143.5 18.3 %collective-permute-start.32 = (f16[2,112,1024]{2,1,0:T(8,128)(2,1)}, f16[2,112,1024]{2,1,0:T(8,128)(2,1)}, u32[]{:S(2)}, u32[]{:S(2)}) collective-permute-start(f16[2,112,1024]{2,1,0:T(8,128)(2,1)} %get-tuple-element.55), channel_id=1, source_target_pairs={{0,1},{4,5},{8,9},{12,13},{16,17},{20,21},{24,25},{28,29}} | collective-permute-start | bytes 1376264 | tf_op jit(solution)/shard_map/ppermute | solution.py:25
  155.0 23.1 %collective-permute-start.35 = (f16[2,112,1024]{2,1,0:T(8,128)(2,1)}, f16[2,112,1024]{2,1,0:T(8,128)(2,1)S(1)}, u32[]{:S(2)}, u32[]{:S(2)}) collective-permute-start(f16[2,112,1024]{2,1,0:T(8,128)(2,1)} %get-tuple-element.56), channel_id=1, source_target_pairs={{3,2},{7,6},{11,10},{15,14},{19,18},{23,22},{27,26},{31,30}} | collective-permute-start | bytes 1376264 | tf_op jit(solution)/shard_map/ppermute | solution.py:26
  159.1 288.4 %all-gather.15.cloned.1.call-start = ((), (), s32[]{:S(2)}) async-start(), calls=%async_computation.4 | async-start | bytes 4128768 | tf_op jit(solution)/shard_map/all_gather | solution.py:66
  160.5 16.5 %collective-permute-start.27 = (f16[2,112,1024]{2,1,0:T(8,128)(2,1)S(1)}, f16[2,112,1024]{2,1,0:T(8,128)(2,1)S(1)}, u32[]{:S(2)}, u32[]{:S(2)}) collective-permute-start(f16[2,112,1024]{2,1,0:T(8,128)(2,1)S(1)} %fusion.52), channel_id=1, source_target_pairs={{0,1},{1,2},{4,5},{5,6},{8,9},{9,10},{12,13},{13,14},{16,17},{17,1... | collective-permute-start | bytes 1376264 | tf_op jit(solution)/shard_map/ppermute | solution.py:25
  163.0 33.6 %collective-permute-start.33 = (f16[2,112,1024]{2,1,0:T(8,128)(2,1)S(1)}, f16[2,112,1024]{2,1,0:T(8,128)(2,1)S(1)}, u32[]{:S(2)}, u32[]{:S(2)}) collective-permute-start(f16[2,112,1024]{2,1,0:T(8,128)(2,1)S(1)} %fusion.47), channel_id=1, source_target_pairs={{0,1},{1,2},{4,5},{5,6},{8,9},{9,10},{12,13},{13,14},{16,17},{17,1... | collective-permute-start | bytes 1376264 | tf_op jit(solution)/shard_map/ppermute | solution.py:25
  171.1 26.0 %copy-start = (f16[2,4,1,112,1024]{4,3,2,1,0:T(8,128)(2,1)}, f16[2,4,1,112,1024]{4,3,2,1,0:T(8,128)(2,1)S(1)}, u32[]{:S(2)}) copy-start(f16[2,4,1,112,1024]{4,3,2,1,0:T(8,128)(2,1)S(1)} %get-tuple-element.27) | copy-start | bytes 5505028
  171.1 25.6 %copy-start.4 = (f16[2,4,1,112,1024]{4,3,2,1,0:T(8,128)(2,1)S(1)}, f16[2,4,1,112,1024]{4,3,2,1,0:T(8,128)(2,1)}, u32[]{:S(2)}) copy-start(f16[2,4,1,112,1024]{4,3,2,1,0:T(8,128)(2,1)} %copy-done.3) | copy-start | bytes 5505028
  171.1 26.7 %copy-start.13 = (bf16[1024,2048]{1,0:T(8,128)(2,1)S(1)}, bf16[1024,2048]{1,0:T(8,128)(2,1)}, u32[]{:S(2)}) copy-start(bf16[1024,2048]{1,0:T(8,128)(2,1)} %all-gather.7.cloned.1.call-done) | copy-start | bytes 12582916
  172.1 94.7 %collective-permute-start.13 = (f16[2,112,1024]{2,1,0:T(8,128)(2,1)}, f16[2,112,1024]{2,1,0:T(8,128)(2,1)}, u32[]{:S(2)}, u32[]{:S(2)}) collective-permute-start(f16[2,112,1024]{2,1,0:T(8,128)(2,1)} %get-tuple-element.43), channel_id=1, source_target_pairs={{0,1},{4,5},{8,9},{12,13},{16,17},{20,21},{24,25},{28,29}} | collective-permute-start | bytes 1376264 | tf_op jit(solution)/shard_map/ppermute | solution.py:25
  177.4 41.1 %collective-permute-start.30 = (f16[2,112,1024]{2,1,0:T(8,128)(2,1)S(1)}, f16[2,112,1024]{2,1,0:T(8,128)(2,1)S(1)}, u32[]{:S(2)}, u32[]{:S(2)}) collective-permute-start(f16[2,112,1024]{2,1,0:T(8,128)(2,1)S(1)} %get-tuple-element.50), channel_id=1, source_target_pairs={{3,2},{2,1},{7,6},{6,5},{11,10},{10,9},{15,14},{14,13},{19,18},{18... | collective-permute-start | bytes 1376264 | tf_op jit(solution)/shard_map/ppermute | solution.py:26
  197.1 23.0 %collective-permute-start.36 = (f16[2,112,1024]{2,1,0:T(8,128)(2,1)S(1)}, f16[2,112,1024]{2,1,0:T(8,128)(2,1)S(1)}, u32[]{:S(2)}, u32[]{:S(2)}) collective-permute-start(f16[2,112,1024]{2,1,0:T(8,128)(2,1)S(1)} %get-tuple-element.54), channel_id=1, source_target_pairs={{3,2},{2,1},{7,6},{6,5},{11,10},{10,9},{15,14},{14,13},{19,18},{18... | collective-permute-start | bytes 1376264 | tf_op jit(solution)/shard_map/ppermute | solution.py:26
  209.0 24.8 %collective-permute-start.28 = (f16[2,112,1024]{2,1,0:T(8,128)(2,1)S(1)}, f16[2,112,1024]{2,1,0:T(8,128)(2,1)S(1)}, u32[]{:S(2)}, u32[]{:S(2)}) collective-permute-start(f16[2,112,1024]{2,1,0:T(8,128)(2,1)S(1)} %get-tuple-element.49), channel_id=1, source_target_pairs={{0,1},{1,2},{2,3},{4,5},{5,6},{6,7},{8,9},{9,10},{10,11},{12,13},{... | collective-permute-start | bytes 1376264 | tf_op jit(solution)/shard_map/ppermute | solution.py:25
  214.0 35.7 %collective-permute-start.34 = (f16[2,112,1024]{2,1,0:T(8,128)(2,1)S(1)}, f16[2,112,1024]{2,1,0:T(8,128)(2,1)S(1)}, u32[]{:S(2)}, u32[]{:S(2)}) collective-permute-start(f16[2,112,1024]{2,1,0:T(8,128)(2,1)S(1)} %get-tuple-element.53), channel_id=1, source_target_pairs={{0,1},{1,2},{2,3},{4,5},{5,6},{6,7},{8,9},{9,10},{10,11},{12,13},{... | collective-permute-start | bytes 1376264 | tf_op jit(solution)/shard_map/ppermute | solution.py:25
  218.8 30.7 %collective-permute-start.31 = (f16[2,112,1024]{2,1,0:T(8,128)(2,1)S(1)}, f16[2,112,1024]{2,1,0:T(8,128)(2,1)S(1)}, u32[]{:S(2)}, u32[]{:S(2)}) collective-permute-start(f16[2,112,1024]{2,1,0:T(8,128)(2,1)S(1)} %fusion.51), channel_id=1, source_target_pairs={{3,2},{2,1},{1,0},{7,6},{6,5},{5,4},{11,10},{10,9},{9,8},{15,14},{... | collective-permute-start | bytes 1376264 | tf_op jit(solution)/shard_map/ppermute | solution.py:26
  220.3 34.7 %collective-permute-start.37 = (f16[2,112,1024]{2,1,0:T(8,128)(2,1)S(1)}, f16[2,112,1024]{2,1,0:T(8,128)(2,1)S(1)}, u32[]{:S(2)}, u32[]{:S(2)}) collective-permute-start(f16[2,112,1024]{2,1,0:T(8,128)(2,1)S(1)} %fusion.46), channel_id=1, source_target_pairs={{3,2},{2,1},{1,0},{7,6},{6,5},{5,4},{11,10},{10,9},{9,8},{15,14},{... | collective-permute-start | bytes 1376264 | tf_op jit(solution)/shard_map/ppermute | solution.py:26
  233.8 80.4 %collective-permute-start.16 = (f16[2,112,1024]{2,1,0:T(8,128)(2,1)S(1)}, f16[2,112,1024]{2,1,0:T(8,128)(2,1)S(1)}, u32[]{:S(2)}, u32[]{:S(2)}) collective-permute-start(f16[2,112,1024]{2,1,0:T(8,128)(2,1)S(1)} %get-tuple-element.44), channel_id=1, source_target_pairs={{3,2},{7,6},{11,10},{15,14},{19,18},{23,22},{27,26},{31,30}} | collective-permute-start | bytes 1376264 | tf_op jit(solution)/shard_map/ppermute | solution.py:26
  257.1 229.1 %all-gather.11.cloned.1.call-start = ((), (), s32[]{:S(2)}) async-start(), calls=%async_computation.2 | async-start | bytes 2293760 | tf_op jit(solution)/shard_map/all_gather | solution.py:75
  257.4 44.2 %copy-start.2 = (f16[2,4,1,112,1024]{4,3,2,1,0:T(8,128)(2,1)S(1)}, f16[2,4,1,112,1024]{4,3,2,1,0:T(8,128)(2,1)}, u32[]{:S(2)}) copy-start(f16[2,4,1,112,1024]{4,3,2,1,0:T(8,128)(2,1)} %get-tuple-element.25) | copy-start | bytes 5505028
  257.4 20.1 %collective-permute-start.19 = (f16[2,112,1024]{2,1,0:T(8,128)(2,1)S(1)}, f16[2,112,1024]{2,1,0:T(8,128)(2,1)S(1)}, u32[]{:S(2)}, u32[]{:S(2)}) collective-permute-start(f16[2,112,1024]{2,1,0:T(8,128)(2,1)S(1)} %get-tuple-element.47), channel_id=1, source_target_pairs={{0,1},{4,5},{8,9},{12,13},{16,17},{20,21},{24,25},{28,29}} | collective-permute-start | bytes 1376264 | tf_op jit(solution)/shard_map/ppermute | solution.py:25
  263.2 70.9 %collective-permute-start.22 = (f16[2,112,1024]{2,1,0:T(8,128)(2,1)S(1)}, f16[2,112,1024]{2,1,0:T(8,128)(2,1)S(1)}, u32[]{:S(2)}, u32[]{:S(2)}) collective-permute-start(f16[2,112,1024]{2,1,0:T(8,128)(2,1)S(1)} %get-tuple-element.48), channel_id=1, source_target_pairs={{3,2},{7,6},{11,10},{15,14},{19,18},{23,22},{27,26},{31,30}} | collective-permute-start | bytes 1376264 | tf_op jit(solution)/shard_map/ppermute | solution.py:26
  265.2 32.0 %collective-permute-start = (f16[2,112,1024]{2,1,0:T(8,128)(2,1)S(1)}, f16[2,112,1024]{2,1,0:T(8,128)(2,1)S(1)}, u32[]{:S(2)}, u32[]{:S(2)}) collective-permute-start(f16[2,112,1024]{2,1,0:T(8,128)(2,1)S(1)} %get-tuple-element.35), channel_id=1, source_target_pairs={{0,1},{4,5},{8,9},{12,13},{16,17},{20,21},{24,25},{28,29}} | collective-permute-start | bytes 1376264 | tf_op jit(solution)/shard_map/ppermute | solution.py:25
  266.7 87.0 %collective-permute-start.3 = (f16[2,112,1024]{2,1,0:T(8,128)(2,1)S(1)}, f16[2,112,1024]{2,1,0:T(8,128)(2,1)S(1)}, u32[]{:S(2)}, u32[]{:S(2)}) collective-permute-start(f16[2,112,1024]{2,1,0:T(8,128)(2,1)S(1)} %get-tuple-element.36), channel_id=1, source_target_pairs={{3,2},{7,6},{11,10},{15,14},{19,18},{23,22},{27,26},{31,30}} | collective-permute-start | bytes 1376264 | tf_op jit(solution)/shard_map/ppermute | solution.py:26
  277.5 32.0 %collective-permute-start.6 = (f16[2,112,1024]{2,1,0:T(8,128)(2,1)S(1)}, f16[2,112,1024]{2,1,0:T(8,128)(2,1)S(1)}, u32[]{:S(2)}, u32[]{:S(2)}) collective-permute-start(f16[2,112,1024]{2,1,0:T(8,128)(2,1)S(1)} %get-tuple-element.39), channel_id=1, source_target_pairs={{0,1},{4,5},{8,9},{12,13},{16,17},{20,21},{24,25},{28,29}} | collective-permute-start | bytes 1376264 | tf_op jit(solution)/shard_map/ppermute | solution.py:25
  297.2 32.0 %collective-permute-start.14 = (f16[2,112,1024]{2,1,0:T(8,128)(2,1)S(1)}, f16[2,112,1024]{2,1,0:T(8,128)(2,1)S(1)}, u32[]{:S(2)}, u32[]{:S(2)}) collective-permute-start(f16[2,112,1024]{2,1,0:T(8,128)(2,1)S(1)} %fusion.62), channel_id=1, source_target_pairs={{0,1},{1,2},{4,5},{5,6},{8,9},{9,10},{12,13},{13,14},{16,17},{17,1... | collective-permute-start | bytes 1376264 | tf_op jit(solution)/shard_map/ppermute | solution.py:25
  309.6 39.3 %collective-permute-start.20 = (f16[2,112,1024]{2,1,0:T(8,128)(2,1)S(1)}, f16[2,112,1024]{2,1,0:T(8,128)(2,1)S(1)}, u32[]{:S(2)}, u32[]{:S(2)}) collective-permute-start(f16[2,112,1024]{2,1,0:T(8,128)(2,1)S(1)} %fusion.57), channel_id=1, source_target_pairs={{0,1},{1,2},{4,5},{5,6},{8,9},{9,10},{12,13},{13,14},{16,17},{17,1... | collective-permute-start | bytes 1376264 | tf_op jit(solution)/shard_map/ppermute | solution.py:25
  314.2 58.2 %collective-permute-start.9 = (f16[2,112,1024]{2,1,0:T(8,128)(2,1)S(1)}, f16[2,112,1024]{2,1,0:T(8,128)(2,1)S(1)}, u32[]{:S(2)}, u32[]{:S(2)}) collective-permute-start(f16[2,112,1024]{2,1,0:T(8,128)(2,1)S(1)} %get-tuple-element.40), channel_id=1, source_target_pairs={{3,2},{7,6},{11,10},{15,14},{19,18},{23,22},{27,26},{31,30}} | collective-permute-start | bytes 1376264 | tf_op jit(solution)/shard_map/ppermute | solution.py:26
  329.2 38.3 %collective-permute-start.1 = (f16[2,112,1024]{2,1,0:T(8,128)(2,1)S(1)}, f16[2,112,1024]{2,1,0:T(8,128)(2,1)S(1)}, u32[]{:S(2)}, u32[]{:S(2)}) collective-permute-start(f16[2,112,1024]{2,1,0:T(8,128)(2,1)S(1)} %fusion.72), channel_id=1, source_target_pairs={{0,1},{1,2},{4,5},{5,6},{8,9},{9,10},{12,13},{13,14},{16,17},{17,1... | collective-permute-start | bytes 1376264 | tf_op jit(solution)/shard_map/ppermute | solution.py:25
  334.1 43.2 %collective-permute-start.7 = (f16[2,112,1024]{2,1,0:T(8,128)(2,1)S(1)}, f16[2,112,1024]{2,1,0:T(8,128)(2,1)S(1)}, u32[]{:S(2)}, u32[]{:S(2)}) collective-permute-start(f16[2,112,1024]{2,1,0:T(8,128)(2,1)S(1)} %fusion.67), channel_id=1, source_target_pairs={{0,1},{1,2},{4,5},{5,6},{8,9},{9,10},{12,13},{13,14},{16,17},{17,1... | collective-permute-start | bytes 1376264 | tf_op jit(solution)/shard_map/ppermute | solution.py:25
  348.9 38.3 %collective-permute-start.15 = (f16[2,112,1024]{2,1,0:T(8,128)(2,1)S(1)}, f16[2,112,1024]{2,1,0:T(8,128)(2,1)S(1)}, u32[]{:S(2)}, u32[]{:S(2)}) collective-permute-start(f16[2,112,1024]{2,1,0:T(8,128)(2,1)S(1)} %get-tuple-element.41), channel_id=1, source_target_pairs={{0,1},{1,2},{2,3},{4,5},{5,6},{6,7},{8,9},{9,10},{10,11},{12,13},{... | collective-permute-start | bytes 1376264 | tf_op jit(solution)/shard_map/ppermute | solution.py:25
  353.7 28.4 %collective-permute-start.17 = (f16[2,112,1024]{2,1,0:T(8,128)(2,1)S(1)}, f16[2,112,1024]{2,1,0:T(8,128)(2,1)S(1)}, u32[]{:S(2)}, u32[]{:S(2)}) collective-permute-start(f16[2,112,1024]{2,1,0:T(8,128)(2,1)S(1)} %get-tuple-element.42), channel_id=1, source_target_pairs={{3,2},{2,1},{7,6},{6,5},{11,10},{10,9},{15,14},{14,13},{19,18},{18... | collective-permute-start | bytes 1376264 | tf_op jit(solution)/shard_map/ppermute | solution.py:26
  367.5 35.1 %collective-permute-start.21 = (f16[2,112,1024]{2,1,0:T(8,128)(2,1)S(1)}, f16[2,112,1024]{2,1,0:T(8,128)(2,1)S(1)}, u32[]{:S(2)}, u32[]{:S(2)}) collective-permute-start(f16[2,112,1024]{2,1,0:T(8,128)(2,1)S(1)} %get-tuple-element.45), channel_id=1, source_target_pairs={{0,1},{1,2},{2,3},{4,5},{5,6},{6,7},{8,9},{9,10},{10,11},{12,13},{... | collective-permute-start | bytes 1376264 | tf_op jit(solution)/shard_map/ppermute | solution.py:25
  372.4 10.7 %collective-permute-start.23 = (f16[2,112,1024]{2,1,0:T(8,128)(2,1)S(1)}, f16[2,112,1024]{2,1,0:T(8,128)(2,1)S(1)}, u32[]{:S(2)}, u32[]{:S(2)}) collective-permute-start(f16[2,112,1024]{2,1,0:T(8,128)(2,1)S(1)} %get-tuple-element.46), channel_id=1, source_target_pairs={{3,2},{2,1},{7,6},{6,5},{11,10},{10,9},{15,14},{14,13},{19,18},{18... | collective-permute-start | bytes 1376264 | tf_op jit(solution)/shard_map/ppermute | solution.py:26
  377.3 36.6 %collective-permute-start.2 = (f16[2,112,1024]{2,1,0:T(8,128)(2,1)S(1)}, f16[2,112,1024]{2,1,0:T(8,128)(2,1)S(1)}, u32[]{:S(2)}, u32[]{:S(2)}) collective-permute-start(f16[2,112,1024]{2,1,0:T(8,128)(2,1)S(1)} %get-tuple-element.33), channel_id=1, source_target_pairs={{0,1},{1,2},{2,3},{4,5},{5,6},{6,7},{8,9},{9,10},{10,11},{12,13},{... | collective-permute-start | bytes 1376264 | tf_op jit(solution)/shard_map/ppermute | solution.py:25
  382.2 2.4 collective-permute-start.4
  383.1 18.5 %collective-permute-start.18 = (f16[2,112,1024]{2,1,0:T(8,128)(2,1)S(1)}, f16[2,112,1024]{2,1,0:T(8,128)(2,1)S(1)}, u32[]{:S(2)}, u32[]{:S(2)}) collective-permute-start(f16[2,112,1024]{2,1,0:T(8,128)(2,1)S(1)} %fusion.61), channel_id=1, source_target_pairs={{3,2},{2,1},{1,0},{7,6},{6,5},{5,4},{11,10},{10,9},{9,8},{15,14},{... | collective-permute-start | bytes 1376264 | tf_op jit(solution)/shard_map/ppermute | solution.py:26
  384.6 25.8 %collective-permute-start.24 = (f16[2,112,1024]{2,1,0:T(8,128)(2,1)S(1)}, f16[2,112,1024]{2,1,0:T(8,128)(2,1)S(1)}, u32[]{:S(2)}, u32[]{:S(2)}) collective-permute-start(f16[2,112,1024]{2,1,0:T(8,128)(2,1)S(1)} %fusion.56), channel_id=1, source_target_pairs={{3,2},{2,1},{1,0},{7,6},{6,5},{5,4},{11,10},{10,9},{9,8},{15,14},{... | collective-permute-start | bytes 1376264 | tf_op jit(solution)/shard_map/ppermute | solution.py:26
  387.2 31.3 %collective-permute-start.8 = (f16[2,112,1024]{2,1,0:T(8,128)(2,1)S(1)}, f16[2,112,1024]{2,1,0:T(8,128)(2,1)S(1)}, u32[]{:S(2)}, u32[]{:S(2)}) collective-permute-start(f16[2,112,1024]{2,1,0:T(8,128)(2,1)S(1)} %get-tuple-element.37), channel_id=1, source_target_pairs={{0,1},{1,2},{2,3},{4,5},{5,6},{6,7},{8,9},{9,10},{10,11},{12,13},{... | collective-permute-start | bytes 1376264 | tf_op jit(solution)/shard_map/ppermute | solution.py:25
  401.6 10.8 %collective-permute-start.10 = (f16[2,112,1024]{2,1,0:T(8,128)(2,1)S(1)}, f16[2,112,1024]{2,1,0:T(8,128)(2,1)S(1)}, u32[]{:S(2)}, u32[]{:S(2)}) collective-permute-start(f16[2,112,1024]{2,1,0:T(8,128)(2,1)S(1)} %get-tuple-element.38), channel_id=1, source_target_pairs={{3,2},{2,1},{7,6},{6,5},{11,10},{10,9},{15,14},{14,13},{19,18},{18... | collective-permute-start | bytes 1376264 | tf_op jit(solution)/shard_map/ppermute | solution.py:26
  402.6 14.7 %collective-permute-start.5 = (f16[2,112,1024]{2,1,0:T(8,128)(2,1)S(1)}, f16[2,112,1024]{2,1,0:T(8,128)(2,1)S(1)}, u32[]{:S(2)}, u32[]{:S(2)}) collective-permute-start(f16[2,112,1024]{2,1,0:T(8,128)(2,1)S(1)} %fusion.71), channel_id=1, source_target_pairs={{3,2},{2,1},{1,0},{7,6},{6,5},{5,4},{11,10},{10,9},{9,8},{15,14},{... | collective-permute-start | bytes 1376264 | tf_op jit(solution)/shard_map/ppermute | solution.py:26
  411.7 5.8 %collective-permute-start.25 = (bf16[224,1024]{1,0:T(8,128)(2,1)S(1)}, bf16[224,1024]{1,0:T(8,128)(2,1)S(1)}, u32[]{:S(2)}, u32[]{:S(2)}) collective-permute-start(bf16[224,1024]{1,0:T(8,128)(2,1)S(1)} %pad_maximum_fusion.2), channel_id=1, source_target_pairs={{0,0},{1,4},{2,8},{3,12},{4,1},{5,5},{6,9},{7,13},{8,2},{9,6},{10,... | collective-permute-start | bytes 1376264 | tf_op jit(solution)/shard_map/ppermute | solution.py:74
  412.6 30.7 %collective-permute-start.11 = (f16[2,112,1024]{2,1,0:T(8,128)(2,1)S(1)}, f16[2,112,1024]{2,1,0:T(8,128)(2,1)S(1)}, u32[]{:S(2)}, u32[]{:S(2)}) collective-permute-start(f16[2,112,1024]{2,1,0:T(8,128)(2,1)S(1)} %fusion.66), channel_id=1, source_target_pairs={{3,2},{2,1},{1,0},{7,6},{6,5},{5,4},{11,10},{10,9},{9,8},{15,14},{... | collective-permute-start | bytes 1376264 | tf_op jit(solution)/shard_map/ppermute | solution.py:26
  418.4 94.3 %all-gather.9.cloned.1.call-start = ((), (), s32[]{:S(2)}) async-start(), calls=%async_computation.1 | async-start | bytes 2293760 | tf_op jit(solution)/shard_map/all_gather | solution.py:75
  445.7 1.0 collective-permute-start.12
  (10 other events, 88.4 us)
Sparse Core Ops, SparseCore 0:
  9.2 39.4 all-gather.12
  50.6 36.7 all-gather.6
  159.2 92.9 all-gather.16
  257.2 109.3 all-gather.14
  418.5 67.6 all-gather.10
  487.6 25.0 all-gather.8

commit v2 on v1

v2 whole, which is shorter than its diff:
```python
import functools

import jax
import jax.numpy as jnp
from jax import lax
from jax.sharding import PartitionSpec as P

HALVES = 2
PIECES = 2
WINDOW = 4
CARRY = jnp.float16


def take(part, owner):
    owner = jnp.clip(owner, 0, part.shape[1] - 1)
    return lax.dynamic_index_in_dim(part, owner, axis=1, keepdims=False).astype(jnp.float32)


def reduce_to_owners(makers, depth):
    me = lax.axis_index("tok")
    total = len(makers) * PIECES
    parts, entry = [], []
    held = [None] * total
    order = []
    for slot in range(total + depth - 2):
        for step in range(1, depth):
            piece = slot - step + 1
            if 0 <= piece < total:
                order.append((piece, step))
    for turn, (piece, step) in enumerate(order):
        if piece == len(parts):
            parts += makers[piece // PIECES](entry[piece - PIECES] if piece else None)
        part = parts[piece]
        rise = take(part, depth - step + me)
        fall = take(part, step - depth + me)
        if step > 1:
            rise = rise + held[piece][0].astype(jnp.float32)
            fall = fall + held[piece][1].astype(jnp.float32)
        rise, fall = rise.astype(CARRY), fall.astype(CARRY)
        if turn >= WINDOW:
            before = order[turn - WINDOW][0]
            rise, fall, *held[before] = lax.optimization_barrier((rise, fall, *held[before]))
        held[piece] = [
            lax.ppermute(rise, "tok", [(i, i + 1) for i in range(step)]),
            lax.ppermute(fall, "tok", [(depth - 1 - i, depth - 2 - i) for i in range(step)]),
        ]
        if step == 1:
            entry.append(held[piece][0])
    return [
        take(part, me) + up.astype(jnp.float32) + down.astype(jnp.float32)
        for part, (up, down) in zip(parts, held)
    ]


def gather_line(block, depth):
    ups, downs = [block], [block]
    for step in range(1, depth):
        ups.append(lax.ppermute(ups[-1], "tok", [(i, i + 1) for i in range(step - 1, depth - 1)]))
        downs.append(
            lax.ppermute(downs[-1], "tok", [(i + 1, i) for i in range(depth - step)])
        )
    line = jnp.concatenate(ups[:0:-1] + downs, axis=0)
    size = block.shape[0]
    start = (depth - 1 - lax.axis_index("tok")) * size
    return lax.dynamic_slice_in_dim(line, start, depth * size, axis=0)


def normalize(summed):
    gate, upward = summed[0], summed[1]
    act = jax.nn.silu(gate) * upward
    inverse = 1.0 / act.shape[1]
    dev = act - jnp.sum(act, axis=1, keepdims=True) * inverse
    spread = jnp.sum(dev * dev, axis=1, keepdims=True) * inverse
    return (dev * lax.rsqrt(spread + 1e-05)).astype(jnp.bfloat16)


def partial_sums(full, weights, half, depth, piece_first, after):
    size = weights.shape[2] // HALVES
    width = size // (depth * PIECES)
    tokens = full.shape[0]
    weights = weights[:, :, half * size : (half + 1) * size]
    if after is not None:
        full, _ = lax.optimization_barrier((full, after))
    part = lax.dot_general(
        weights, full, (((0,), (1,)), ((), ())), preferred_element_type=jnp.float32
    ).astype(CARRY)
    if piece_first:
        part = part.reshape(2, PIECES, depth, width, tokens)
        return [part[:, q] for q in range(PIECES)]
    part = part.reshape(2, depth, PIECES, width, tokens)
    return [part[:, :, q] for q in range(PIECES)]


def local(first_inputs, second_inputs, first_weights, second_weights):
    depth = lax.axis_size("tok")
    wide = lax.axis_size("col")
    rows = lax.axis_size("row")
    full_second = lax.all_gather(second_inputs, ("row", "col"), axis=0, tiled=True)
    full_first = lax.all_gather(first_inputs, ("row", "col"), axis=0, tiled=True)
    tokens = full_first.shape[0]
    makers = [
        functools.partial(partial_sums, full, weights, half, depth, piece_first)
        for full, weights, piece_first in (
            (full_second, second_weights, False),
            (full_first, first_weights, True),
        )
        for half in range(HALVES)
    ]
    norms = [normalize(summed) for summed in reduce_to_owners(makers, depth)]
    count = HALVES * PIECES
    second = []
    for half in range(HALVES):
        norm = jnp.concatenate(norms[half * PIECES : (half + 1) * PIECES], axis=0)
        norm = gather_line(norm, depth)
        norm = lax.all_gather(norm, "row", axis=0, tiled=True)
        second.append(norm.reshape(rows, -1, tokens))
    second = jnp.concatenate(second, axis=1).reshape(-1, tokens)
    first = []
    for norm in norms[count:]:
        if wide == depth:
            swap = [(c * depth + t, t * depth + c) for c in range(wide) for t in range(depth)]
            norm = lax.ppermute(norm, ("col", "tok"), swap)
            norm = lax.all_gather(norm, "col", axis=0, tiled=True)
        else:
            norm = lax.all_gather(norm, ("col", "tok"), axis=0, tiled=True)
            norm = norm.reshape(wide, -1, tokens)
        first.append(norm)
    if wide == depth:
        first = jnp.concatenate(first, axis=0)
    else:
        first = jnp.concatenate(first, axis=1).reshape(-1, tokens)
        share = first.shape[0] // depth
        first = lax.dynamic_slice_in_dim(first, lax.axis_index("tok") * share, share, axis=0)
    total = lax.dot_general(
        first, second, (((1,), (1,)), ((), ())), preferred_element_type=jnp.float32
    )
    return total * float(tokens) ** (-0.5)


def solution(mesh):
    placed = (
        P(("row", "col"), "tok"),
        P(("row", "col"), "tok"),
        P("tok", None, ("row", "col")),
        P("tok", None, ("col", "row")),
    )
    return jax.shard_map(
        local, mesh=mesh, in_specs=placed, out_specs=P(("row", "tok"), "col"), check_vma=False
    )
```

time: 550 us -> 506 us (0.920)
  waiting for transfers between devices: 251 us -> 120 us
  blocking collectives: 0 us -> 52.6 us
  starting transfers between devices: 129 us -> 155 us
  other arithmetic: 32.8 us -> 42.8 us
    ppermute x48 -> x60, waiting for transfers between devices: 163 us -> 90.6 us  [the longest x24 48.3 us: reduce_to_owners(): lax.ppermute(rise, 'tok', [(i, i + 1) for i in range(step)])]
    all_gather x4 -> x2, waiting for transfers between devices: 58.4 us -> 0.01 us  [local(): norm = lax.all_gather(norm, 'row', axis=0, tiled=True)]
    all_gather x0 -> x4, blocking collectives: none -> 52.6 us  [local(): norm = lax.all_gather(norm, 'col', axis=0, tiled=True)]
    ppermute x48 -> x60, starting transfers between devices: 127 us -> 151 us  [the longest x24 104 us: reduce_to_owners(): lax.ppermute(rise, 'tok', [(i, i + 1) for i in range(step)])]
    convert_element_type x24 -> x15, other arithmetic: 14.6 us -> 23.1 us  [reduce_to_owners(): rise, fall = (rise.astype(CARRY), fall.astype(CARRY))]
  transfers between devices with their start and end apart: 56 -> 68, of which waited for: 20 -> 15; matrix products, arithmetic and copies ran while one was open for 22% -> 25% of each run, Pallas kernels for 0% -> 0%
where the time goes in v2:
time: 506 us; the launch traced here: 498 us
  starting transfers between devices  155 us (31%)
  waiting for transfers between devices  120 us (24%)
  matrix products  67.5 us (13%)
  blocking collectives  52.6 us (10%)
  local copies, waits for them, and re-layouts  46.2 us (9%)
  other arithmetic  42.8 us (8%)
  between operations  14.9 us (3%)
    ppermute x24, starting transfers between devices, reduce_to_owners(): lax.ppermute(rise, 'tok', [(i, i + 1) for i in range(step)])  104 us
    all_gather x4, blocking collectives, local(): norm = lax.all_gather(norm, 'col', axis=0, tiled=True)  52.6 us
    ppermute x24, waiting for transfers between devices, reduce_to_owners(): lax.ppermute(rise, 'tok', [(i, i + 1) for i in range(step)])  48.3 us
    dot_general x4, matrix products, partial_sums(): lax.dot_general(weights, full, (((0,), (1,)), ((), ())), preferred_elemen...  46.6 us
    ppermute x6, waiting for transfers between devices, gather_line(): lax.ppermute(downs[-1], 'tok', [(i + 1, i) for i in range(depth - step)])  33.8 us
    all_gather x1, waiting for transfers between devices, local(): lax.all_gather(second_inputs, ('row', 'col'), axis=0, tiled=True)  27.8 us
    ppermute x24, starting transfers between devices, reduce_to_owners(): lax.ppermute(fall, 'tok', [(depth - 1 - i, depth - 2 - i) for i in range(...  26.9 us
    slice x2, local copies, waits for them, and re-layouts, partial_sums(): weights = weights[:, :, half * size:(half + 1) * size]  24.4 us
  transfers between devices with their start and end apart: 68, of which 15 were waited for; matrix products, arithmetic and copies ran while one was open for 25% of the time, Pallas kernels for 0%

profile of v2, /device:TPU:0, one launch (start us, length us, event | category | flops | bytes accessed | tf_op | source)
XLA Modules:
  0.0 498.4 jit_solution(9481529586646405037)
XLA Ops:
  8.1 12.8 %fusion.104 = (bf16[2048,2,896]{2,1,0:T(2,128)(2,1)}, bf16[2048,2,896]{2,1,0:T(2,128)(2,1)}) fusion(bf16[2048,2,1792]{2,1,0:T(2,128)(2,1)} %param.7), kind=kLoop, calls=%fused_computation.206 | loop fusion | bytes 29360128 | tf_op jit(solution)/shard_map/slice | solution.py:81
  20.9 27.8 %all-gather.7.cloned.1.call-done = bf16[1024,2048]{1,0:T(8,128)(2,1)} async-done(((bf16[128,2048]{1,0:T(8,128)(2,1)}), bf16[1024,2048]{1,0:T(8,128)(2,1)}) %all-gather.7.cloned.1.call-update) | async-done | bytes 4194320 | tf_op jit(solution)/shard_map/all_gather | solution.py:98
  48.7 11.8 %fusion.19 = f16[2,896,1024]{2,1,0:T(8,128)(2,1)S(1)} fusion(bf16[1024,2048]{1,0:T(8,128)(2,1)} %all-gather.7.cloned.1.call-done, bf16[2048,2,896]{2,1,0:T(2,128)(2,1)} %get-tuple-element.147), kind=kOutput, calls=%fused_computation.21 | convolution fusion | flops 7518027776 | bytes 15204352 | tf_op jit(solution)/shard_map/dot_general | solution.py:84
  60.5 2.6 fusion.108
  64.4 3.4 collective-permute-start
  68.5 2.1 dynamic-slice_bitcast_fusion.8
  73.4 5.6 %collective-permute-done = f16[2,112,1024]{2,1,0:T(8,128)(2,1)S(1)} collective-permute-done((f16[2,112,1024]{2,1,0:T(8,128)(2,1)}, f16[2,112,1024]{2,1,0:T(8,128)(2,1)S(1)}, u32[]{:S(2)}, u32[]{:S(2)}) %collective-permute-start) | collective-permute-done | bytes 458784 | tf_op jit(solution)/shard_map/ppermute | solution.py:44
  80.4 4.3 collective-permute-start.4
  85.6 13.2 %fusion.24 = f16[1024,2,896]{0,2,1:T(8,128)(2,1)} fusion(bf16[2048,2,896]{2,1,0:T(2,128)(2,1)} %get-tuple-element.148, bf16[1024,2048]{1,0:T(8,128)(2,1)} %all-gather.7.cloned.1.call-done), kind=kOutput, calls=%fused_computation.22 | convolution fusion | flops 7518027776 | bytes 15204352 | tf_op jit(solution)/shard_map/dot_general | solution.py:84
  98.8 3.1 fusion.109
  104.4 5.4 %collective-permute-start.1 = (f16[2,112,1024]{2,1,0:T(8,128)(2,1)}, f16[2,112,1024]{2,1,0:T(8,128)(2,1)}, u32[]{:S(2)}, u32[]{:S(2)}) collective-permute-start(f16[2,112,1024]{2,1,0:T(8,128)(2,1)} %get-tuple-element.184), channel_id=1, source_target_pairs={{0,1},{4,5},{8,9},{12,13},{16,17},{20,21},{24,25},{28,29}} | collective-permute-start | bytes 1376264 | tf_op jit(solution)/shard_map/ppermute | solution.py:44
  111.2 11.6 %fusion.105 = (bf16[2048,2,896]{2,1,0:T(2,128)(2,1)}, bf16[2048,2,896]{2,1,0:T(2,128)(2,1)}) fusion(bf16[2048,2,1792]{2,1,0:T(2,128)(2,1)S(1)} %bitcast.373), kind=kLoop, calls=%fused_computation.207 | loop fusion | bytes 29360128 | tf_op jit(solution)/shard_map/slice | solution.py:81
  123.9 2.7 fusion.75
  129.3 1.9 fusion.48
  131.2 3.7 collective-permute-start.36
  136.0 11.8 %fusion.29 = f16[1024,2,896]{0,2,1:T(8,128)(2,1)S(1)} fusion(bf16[2048,2,896]{2,1,0:T(2,128)(2,1)} %get-tuple-element.149, bf16[1024,2048]{1,0:T(8,128)(2,1)} %all-gather.5.cloned.1.call-done), kind=kOutput, calls=%fused_computation.23 | convolution fusion | flops 7518027776 | bytes 15204352 | tf_op jit(solution)/shard_map/dot_general | solution.py:84
  149.8 1.6 collective-permute-start.10
  151.4 5.8 %collective-permute-start.9 = (f16[2,112,1024]{2,1,0:T(8,128)(2,1)S(1)}, f16[2,112,1024]{2,1,0:T(8,128)(2,1)S(1)}, u32[]{:S(2)}, u32[]{:S(2)}) collective-permute-start(f16[2,112,1024]{2,1,0:T(8,128)(2,1)S(1)} %get-tuple-element.74), channel_id=1, source_target_pairs={{0,1},{1,2},{2,3},{4,5},{5,6},{6,7},{8,9},{9,10},{10,11},{12,13},{... | collective-permute-start | bytes 1376264 | tf_op jit(solution)/shard_map/ppermute | solution.py:44
  158.7 4.5 collective-permute-start.26
  168.0 5.5 %collective-permute-start.38 = (f16[2,112,1024]{2,1,0:T(8,128)(2,1)}, f16[2,112,1024]{2,1,0:T(8,128)(2,1)}, u32[]{:S(2)}, u32[]{:S(2)}) collective-permute-start(f16[2,112,1024]{2,1,0:T(8,128)(2,1)} %get-tuple-element.107), channel_id=1, source_target_pairs={{0,1},{1,2},{2,3},{4,5},{5,6},{6,7},{8,9},{9,10},{10,11},{12,13},{... | collective-permute-start | bytes 1376264 | tf_op jit(solution)/shard_map/ppermute | solution.py:44
  173.5 3.2 collective-permute-start.11
  178.1 5.1 %collective-permute-start.28 = (f16[2,112,1024]{2,1,0:T(8,128)(2,1)}, f16[2,112,1024]{2,1,0:T(8,128)(2,1)}, u32[]{:S(2)}, u32[]{:S(2)}) collective-permute-start(f16[2,112,1024]{2,1,0:T(8,128)(2,1)} %get-tuple-element.99), channel_id=1, source_target_pairs={{0,1},{4,5},{8,9},{12,13},{16,17},{20,21},{24,25},{28,29}} | collective-permute-start | bytes 1376264 | tf_op jit(solution)/shard_map/ppermute | solution.py:44
  187.1 10.5 %collective-permute-done.11 = f16[2,112,1024]{2,1,0:T(8,128)(2,1)S(1)} collective-permute-done((f16[2,112,1024]{2,1,0:T(8,128)(2,1)S(1)}, f16[2,112,1024]{2,1,0:T(8,128)(2,1)S(1)}, u32[]{:S(2)}, u32[]{:S(2)}) %collective-permute-start.11) | collective-permute-done | bytes 458784 | tf_op jit(solution)/shard_map/ppermute | solution.py:44
  197.6 5.3 %collective-permute-start.12 = (f16[2,112,1024]{2,1,0:T(8,128)(2,1)}, f16[2,112,1024]{2,1,0:T(8,128)(2,1)}, u32[]{:S(2)}, u32[]{:S(2)}) collective-permute-start(f16[2,112,1024]{2,1,0:T(8,128)(2,1)} %get-tuple-element.80), channel_id=1, source_target_pairs={{0,1},{4,5},{8,9},{12,13},{16,17},{20,21},{24,25},{28,29}} | collective-permute-start | bytes 1376264 | tf_op jit(solution)/shard_map/ppermute | solution.py:44
  203.0 9.7 %fusion.34 = f16[1024,2,896]{0,2,1:T(8,128)(2,1)S(1)} fusion(bf16[2048,2,896]{2,1,0:T(2,128)(2,1)S(1)} %bitcast.375, bf16[1024,2048]{1,0:T(8,128)(2,1)} %all-gather.5.cloned.1.call-done), kind=kOutput, calls=%fused_computation.24 | convolution fusion | flops 7518027776 | bytes 15204352 | tf_op jit(solution)/shard_map/dot_general | solution.py:84
  213.4 1.6 fusion.63
  216.3 4.6 collective-permute-start.52
  220.9 1.9 collective-permute-start.21
  222.8 1.6 fusion.56
  226.6 2.5 collective-permute-start.30
  229.8 2.3 collective-permute-done.52
  232.1 4.3 collective-permute-start.14
  236.4 5.4 %collective-permute-done.21 = f16[2,112,1024]{2,1,0:T(8,128)(2,1)S(1)} collective-permute-done((f16[2,112,1024]{2,1,0:T(8,128)(2,1)S(1)}, f16[2,112,1024]{2,1,0:T(8,128)(2,1)S(1)}, u32[]{:S(2)}, u32[]{:S(2)}) %collective-permute-start.21) | collective-permute-done | bytes 458784 | tf_op jit(solution)/shard_map/ppermute | solution.py:44
  245.2 11.7 %collective-permute-done.14 = f16[2,112,1024]{2,1,0:T(8,128)(2,1)S(1)} collective-permute-done((f16[2,112,1024]{2,1,0:T(8,128)(2,1)S(1)}, f16[2,112,1024]{2,1,0:T(8,128)(2,1)S(1)}, u32[]{:S(2)}, u32[]{:S(2)}) %collective-permute-start.14) | collective-permute-done | bytes 458784 | tf_op jit(solution)/shard_map/ppermute | solution.py:44
  256.9 4.4 collective-permute-start.40
  263.2 2.2 collective-permute-start.16
  265.3 1.8 fusion.55
  268.4 3.8 collective-permute-done.40
  272.2 4.4 collective-permute-start.32
  283.1 6.0 %collective-permute-start.23 = (f16[2,112,1024]{2,1,0:T(8,128)(2,1)}, f16[2,112,1024]{2,1,0:T(8,128)(2,1)}, u32[]{:S(2)}, u32[]{:S(2)}) collective-permute-start(f16[2,112,1024]{2,1,0:T(8,128)(2,1)} %get-tuple-element.91), channel_id=1, source_target_pairs={{0,1},{1,2},{2,3},{4,5},{5,6},{6,7},{8,9},{9,10},{10,11},{12,13},{... | collective-permute-start | bytes 1376264 | tf_op jit(solution)/shard_map/ppermute | solution.py:44
  291.2 5.2 %collective-permute-start.42 = (f16[2,112,1024]{2,1,0:T(8,128)(2,1)}, f16[2,112,1024]{2,1,0:T(8,128)(2,1)}, u32[]{:S(2)}, u32[]{:S(2)}) collective-permute-start(f16[2,112,1024]{2,1,0:T(8,128)(2,1)} %get-tuple-element.111), channel_id=1, source_target_pairs={{0,1},{1,2},{4,5},{5,6},{8,9},{9,10},{12,13},{13,14},{16,17},{17,1... | collective-permute-start | bytes 1376264 | tf_op jit(solution)/shard_map/ppermute | solution.py:44
  297.7 4.2 collective-permute-done.56
  302.0 1.5 collective-permute-start.43
  305.6 8.3 %collective-permute-done.57 = bf16[224,1024]{1,0:T(8,128)(2,1)S(1)} collective-permute-done((bf16[224,1024]{1,0:T(8,128)(2,1)S(1)}, bf16[224,1024]{1,0:T(8,128)(2,1)S(1)}, u32[]{:S(2)}, u32[]{:S(2)}) %collective-permute-start.57) | collective-permute-done | bytes 458784 | tf_op jit(solution)/shard_map/ppermute | solution.py:60
  313.9 2.2 collective-permute-start.18
  317.6 1.6 fusion.39
  321.7 2.7 fusion.45
  324.6 4.9 collective-permute-start.58
  329.5 12.6 %all_gather.27 = bf16[448,1024]{1,0:T(8,128)(2,1)S(1)} all-gather(bf16[112,1024]{1,0:T(8,128)(2,1)S(1)} %collective-permute-done.34), channel_id=1, replica_groups=mesh['row'=2,'col'=4,'tok'=4] {'col'}, dimensions={0}, use_global_device_ids=true | all-gather | bytes 1146880 | tf_op jit(solution)/shard_map/all_gather | solution.py:123
  345.6 1.6 fusion.78
  347.4 7.1 %collective-permute-start.44 = (f16[2,112,1024]{2,1,0:T(8,128)(2,1)S(1)}, f16[2,112,1024]{2,1,0:T(8,128)(2,1)S(1)}, u32[]{:S(2)}, u32[]{:S(2)}) collective-permute-start(f16[2,112,1024]{2,1,0:T(8,128)(2,1)S(1)} %get-tuple-element.113), channel_id=1, source_target_pairs={{0,1},{1,2},{4,5},{5,6},{8,9},{9,10},{12,13},{13,14},{16,17},{17,1... | collective-permute-start | bytes 1376264 | tf_op jit(solution)/shard_map/ppermute | solution.py:44
  355.2 1.5 collective-permute-done.61
  360.4 3.8 collective-permute-done.44
  364.2 13.4 %collective-permute-start.46 = (f16[2,112,1024]{2,1,0:T(8,128)(2,1)}, f16[2,112,1024]{2,1,0:T(8,128)(2,1)}, u32[]{:S(2)}, u32[]{:S(2)}) collective-permute-start(f16[2,112,1024]{2,1,0:T(8,128)(2,1)} %get-tuple-element.117), channel_id=1, source_target_pairs={{0,1},{1,2},{2,3},{4,5},{5,6},{6,7},{8,9},{9,10},{10,11},{12,13},{... | collective-permute-start | bytes 1376264 | tf_op jit(solution)/shard_map/ppermute | solution.py:44
  380.7 19.8 %collective-permute-done.63 = bf16[224,1024]{1,0:T(8,128)(2,1)S(1)} collective-permute-done((bf16[224,1024]{1,0:T(8,128)(2,1)S(1)}, bf16[224,1024]{1,0:T(8,128)(2,1)S(1)}, u32[]{:S(2)}, u32[]{:S(2)}) %collective-permute-start.63) | collective-permute-done | bytes 458784 | tf_op jit(solution)/shard_map/ppermute | solution.py:60
  401.9 9.7 %all_gather.26 = bf16[448,1024]{1,0:T(8,128)(2,1)} all-gather(bf16[112,1024]{1,0:T(8,128)(2,1)} %collective-permute-done.25), channel_id=1, replica_groups=mesh['row'=2,'col'=4,'tok'=4] {'col'}, dimensions={0}, use_global_device_ids=true | all-gather | bytes 1146880 | tf_op jit(solution)/shard_map/all_gather | solution.py:123
  413.2 1.5 collective-permute-start.49
  416.0 1.6 fusion.54
  418.8 6.7 %collective-permute-done.49 = f16[2,112,1024]{2,1,0:T(8,128)(2,1)S(1)} collective-permute-done((f16[2,112,1024]{2,1,0:T(8,128)(2,1)S(1)}, f16[2,112,1024]{2,1,0:T(8,128)(2,1)S(1)}, u32[]{:S(2)}, u32[]{:S(2)}) %collective-permute-start.49) | collective-permute-done | bytes 458784 | tf_op jit(solution)/shard_map/ppermute | solution.py:44
  425.5 6.1 %collective-permute-done.50 = f16[2,112,1024]{2,1,0:T(8,128)(2,1)S(1)} collective-permute-done((f16[2,112,1024]{2,1,0:T(8,128)(2,1)S(1)}, f16[2,112,1024]{2,1,0:T(8,128)(2,1)S(1)}, u32[]{:S(2)}, u32[]{:S(2)}) %collective-permute-start.50) | collective-permute-done | bytes 458784 | tf_op jit(solution)/shard_map/ppermute | solution.py:45
  433.2 20.2 %all_gather.28 = bf16[448,1024]{1,0:T(8,128)(2,1)S(1)} all-gather(bf16[112,1024]{1,0:T(8,128)(2,1)S(1)} %collective-permute-done.48), channel_id=1, replica_groups=mesh['row'=2,'col'=4,'tok'=4] {'col'}, dimensions={0}, use_global_device_ids=true | all-gather | bytes 1146880 | tf_op jit(solution)/shard_map/all_gather | solution.py:123
  453.4 10.1 %all_gather.29 = bf16[448,1024]{1,0:T(8,128)(2,1)} all-gather(bf16[112,1024]{1,0:T(8,128)(2,1)S(1)} %collective-permute-done.51), channel_id=1, replica_groups=mesh['row'=2,'col'=4,'tok'=4] {'col'}, dimensions={0}, use_global_device_ids=true | all-gather | bytes 1146880 | tf_op jit(solution)/shard_map/all_gather | solution.py:123
  463.5 7.0 %pad_maximum_fusion = bf16[2,1792,1024]{2,1,0:T(8,128)(2,1)} fusion(bf16[2,896,1024]{2,1,0:T(8,128)(2,1)} %bitcast.378, bf16[2,896,1024]{2,1,0:T(8,128)(2,1)} %bitcast.377), kind=kLoop, calls=%fused_computation.1 | loop fusion | flops 14680064 | bytes 14680064 | tf_op jit(solution)/shard_map/concatenate | solution.py:117
  470.5 20.9 %convolution_multiply_fusion = f32[1792,3584]{1,0:T(8,128)} fusion(bf16[3584,1024]{1,0:T(8,128)(2,1)} %bitcast.376, bf16[448,1024]{1,0:T(8,128)(2,1)} %all_gather.29, bf16[448,1024]{1,0:T(8,128)(2,1)S(1)} %all_gather.28, bf16[448,1024]{1,0:T(8,128)(2,1)S(1)} %all_gather.27, bf16[448,1024]{1,0:T(8,128)(2,1)S(1)} %copy-done.10), kind=kOutput, calls=%fused_computation | convolution fusion | flops 13174439936 | bytes 36700160 | tf_op jit(solution)/shard_map/dot_general | solution.py:134
  (229 shorter events, 75.9 us)
Async XLA Ops:
  6.5 42.2 %all-gather.7.cloned.1.call-start = ((), (), s32[]{:S(2)}) async-start(), calls=%async_computation.1 | async-start | bytes 4718592 | tf_op jit(solution)/shard_map/all_gather | solution.py:98
  7.3 122.1 %all-gather.5.cloned.1.call-start = ((), (), s32[]{:S(2)}) async-start(), calls=%async_computation | async-start | bytes 4718592 | tf_op jit(solution)/shard_map/all_gather | solution.py:99
  8.0 455.5 %all-gather.9.cloned.1.call-start = ((), (), s32[]{:S(2)}) async-start(), calls=%async_computation.2 | async-start | bytes 5505024 | tf_op jit(solution)/shard_map/all_gather | solution.py:115
  64.4 14.6 %collective-permute-start = (f16[2,112,1024]{2,1,0:T(8,128)(2,1)}, f16[2,112,1024]{2,1,0:T(8,128)(2,1)S(1)}, u32[]{:S(2)}, u32[]{:S(2)}) collective-permute-start(f16[2,112,1024]{2,1,0:T(8,128)(2,1)} %get-tuple-element.198), channel_id=1, source_target_pairs={{0,1},{4,5},{8,9},{12,13},{16,17},{20,21},{24,25},{28,29}} | collective-permute-start | bytes 1376264 | tf_op jit(solution)/shard_map/ppermute | solution.py:44
  67.8 11.1 %collective-permute-start.5 = (f16[2,112,1024]{2,1,0:T(8,128)(2,1)}, f16[2,112,1024]{2,1,0:T(8,128)(2,1)S(1)}, u32[]{:S(2)}, u32[]{:S(2)}) collective-permute-start(f16[2,112,1024]{2,1,0:T(8,128)(2,1)} %get-tuple-element.197), channel_id=1, source_target_pairs={{3,2},{7,6},{11,10},{15,14},{19,18},{23,22},{27,26},{31,30}} | collective-permute-start | bytes 1376264 | tf_op jit(solution)/shard_map/ppermute | solution.py:45
  70.6 39.1 %collective-permute-start.2 = (f16[2,112,1024]{2,1,0:T(8,128)(2,1)S(1)}, f16[2,112,1024]{2,1,0:T(8,128)(2,1)S(1)}, u32[]{:S(2)}, u32[]{:S(2)}) collective-permute-start(f16[2,112,1024]{2,1,0:T(8,128)(2,1)S(1)} %get-tuple-element.202), channel_id=1, source_target_pairs={{0,1},{4,5},{8,9},{12,13},{16,17},{20,21},{24,25},{28,29}} | collective-permute-start | bytes 1376264 | tf_op jit(solution)/shard_map/ppermute | solution.py:44
  71.9 51.9 %collective-permute-start.3 = (f16[2,112,1024]{2,1,0:T(8,128)(2,1)}, f16[2,112,1024]{2,1,0:T(8,128)(2,1)}, u32[]{:S(2)}, u32[]{:S(2)}) collective-permute-start(f16[2,112,1024]{2,1,0:T(8,128)(2,1)} %get-tuple-element.201), channel_id=1, source_target_pairs={{3,2},{7,6},{11,10},{15,14},{19,18},{23,22},{27,26},{31,30}} | collective-permute-start | bytes 1376264 | tf_op jit(solution)/shard_map/ppermute | solution.py:45
  80.4 46.2 %collective-permute-start.4 = (f16[2,112,1024]{2,1,0:T(8,128)(2,1)}, f16[2,112,1024]{2,1,0:T(8,128)(2,1)S(1)}, u32[]{:S(2)}, u32[]{:S(2)}) collective-permute-start(f16[2,112,1024]{2,1,0:T(8,128)(2,1)} %get-tuple-element.196), channel_id=1, source_target_pairs={{0,1},{1,2},{4,5},{5,6},{8,9},{9,10},{12,13},{13,14},{16,17},{17,1... | collective-permute-start | bytes 1376264 | tf_op jit(solution)/shard_map/ppermute | solution.py:44
  84.7 41.9 %collective-permute-start.6 = (f16[2,112,1024]{2,1,0:T(8,128)(2,1)}, f16[2,112,1024]{2,1,0:T(8,128)(2,1)S(1)}, u32[]{:S(2)}, u32[]{:S(2)}) collective-permute-start(f16[2,112,1024]{2,1,0:T(8,128)(2,1)} %get-tuple-element.195), channel_id=1, source_target_pairs={{3,2},{2,1},{7,6},{6,5},{11,10},{10,9},{15,14},{14,13},{19,18},{18... | collective-permute-start | bytes 1376264 | tf_op jit(solution)/shard_map/ppermute | solution.py:45
  104.4 25.0 %collective-permute-start.1 = (f16[2,112,1024]{2,1,0:T(8,128)(2,1)}, f16[2,112,1024]{2,1,0:T(8,128)(2,1)}, u32[]{:S(2)}, u32[]{:S(2)}) collective-permute-start(f16[2,112,1024]{2,1,0:T(8,128)(2,1)} %get-tuple-element.184), channel_id=1, source_target_pairs={{0,1},{4,5},{8,9},{12,13},{16,17},{20,21},{24,25},{28,29}} | collective-permute-start | bytes 1376264 | tf_op jit(solution)/shard_map/ppermute | solution.py:44
  109.7 19.6 %collective-permute-start.35 = (f16[2,112,1024]{2,1,0:T(8,128)(2,1)}, f16[2,112,1024]{2,1,0:T(8,128)(2,1)}, u32[]{:S(2)}, u32[]{:S(2)}) collective-permute-start(f16[2,112,1024]{2,1,0:T(8,128)(2,1)} %get-tuple-element.183), channel_id=1, source_target_pairs={{3,2},{7,6},{11,10},{15,14},{19,18},{23,22},{27,26},{31,30}} | collective-permute-start | bytes 1376264 | tf_op jit(solution)/shard_map/ppermute | solution.py:45
  126.6 23.3 %collective-permute-start.7 = (f16[2,112,1024]{2,1,0:T(8,128)(2,1)}, f16[2,112,1024]{2,1,0:T(8,128)(2,1)S(1)}, u32[]{:S(2)}, u32[]{:S(2)}) collective-permute-start(f16[2,112,1024]{2,1,0:T(8,128)(2,1)} %get-tuple-element.72), channel_id=1, source_target_pairs={{0,1},{1,2},{4,5},{5,6},{8,9},{9,10},{12,13},{13,14},{16,17},{17,1... | collective-permute-start | bytes 1376264 | tf_op jit(solution)/shard_map/ppermute | solution.py:44
  127.9 21.9 %collective-permute-start.8 = (f16[2,112,1024]{2,1,0:T(8,128)(2,1)}, f16[2,112,1024]{2,1,0:T(8,128)(2,1)}, u32[]{:S(2)}, u32[]{:S(2)}) collective-permute-start(f16[2,112,1024]{2,1,0:T(8,128)(2,1)} %get-tuple-element.73), channel_id=1, source_target_pairs={{3,2},{2,1},{7,6},{6,5},{11,10},{10,9},{15,14},{14,13},{19,18},{18... | collective-permute-start | bytes 1376264 | tf_op jit(solution)/shard_map/ppermute | solution.py:45
  131.2 32.0 %collective-permute-start.36 = (f16[2,112,1024]{2,1,0:T(8,128)(2,1)S(1)}, f16[2,112,1024]{2,1,0:T(8,128)(2,1)S(1)}, u32[]{:S(2)}, u32[]{:S(2)}) collective-permute-start(f16[2,112,1024]{2,1,0:T(8,128)(2,1)S(1)} %get-tuple-element.105), channel_id=1, source_target_pairs={{0,1},{1,2},{4,5},{5,6},{8,9},{9,10},{12,13},{13,14},{16,17},{17,1... | collective-permute-start | bytes 1376264 | tf_op jit(solution)/shard_map/ppermute | solution.py:44
  134.9 31.7 %collective-permute-start.37 = (f16[2,112,1024]{2,1,0:T(8,128)(2,1)S(1)}, f16[2,112,1024]{2,1,0:T(8,128)(2,1)S(1)}, u32[]{:S(2)}, u32[]{:S(2)}) collective-permute-start(f16[2,112,1024]{2,1,0:T(8,128)(2,1)S(1)} %get-tuple-element.106), channel_id=1, source_target_pairs={{3,2},{2,1},{7,6},{6,5},{11,10},{10,9},{15,14},{14,13},{19,18},{18... | collective-permute-start | bytes 1376264 | tf_op jit(solution)/shard_map/ppermute | solution.py:45
  149.8 23.6 %collective-permute-start.10 = (f16[2,112,1024]{2,1,0:T(8,128)(2,1)S(1)}, f16[2,112,1024]{2,1,0:T(8,128)(2,1)S(1)}, u32[]{:S(2)}, u32[]{:S(2)}) collective-permute-start(f16[2,112,1024]{2,1,0:T(8,128)(2,1)S(1)} %get-tuple-element.75), channel_id=1, source_target_pairs={{3,2},{2,1},{1,0},{7,6},{6,5},{5,4},{11,10},{10,9},{9,8},{15,14},{... | collective-permute-start | bytes 1376264 | tf_op jit(solution)/shard_map/ppermute | solution.py:45
  151.4 22.1 %collective-permute-start.9 = (f16[2,112,1024]{2,1,0:T(8,128)(2,1)S(1)}, f16[2,112,1024]{2,1,0:T(8,128)(2,1)S(1)}, u32[]{:S(2)}, u32[]{:S(2)}) collective-permute-start(f16[2,112,1024]{2,1,0:T(8,128)(2,1)S(1)} %get-tuple-element.74), channel_id=1, source_target_pairs={{0,1},{1,2},{2,3},{4,5},{5,6},{6,7},{8,9},{9,10},{10,11},{12,13},{... | collective-permute-start | bytes 1376264 | tf_op jit(solution)/shard_map/ppermute | solution.py:44
  158.7 19.5 %collective-permute-start.26 = (f16[2,112,1024]{2,1,0:T(8,128)(2,1)S(1)}, f16[2,112,1024]{2,1,0:T(8,128)(2,1)S(1)}, u32[]{:S(2)}, u32[]{:S(2)}) collective-permute-start(f16[2,112,1024]{2,1,0:T(8,128)(2,1)S(1)} %get-tuple-element.97), channel_id=1, source_target_pairs={{0,1},{1,2},{2,3},{4,5},{5,6},{6,7},{8,9},{9,10},{10,11},{12,13},{... | collective-permute-start | bytes 1376264 | tf_op jit(solution)/shard_map/ppermute | solution.py:44
  163.2 14.9 %collective-permute-start.27 = (f16[2,112,1024]{2,1,0:T(8,128)(2,1)S(1)}, f16[2,112,1024]{2,1,0:T(8,128)(2,1)S(1)}, u32[]{:S(2)}, u32[]{:S(2)}) collective-permute-start(f16[2,112,1024]{2,1,0:T(8,128)(2,1)S(1)} %get-tuple-element.98), channel_id=1, source_target_pairs={{3,2},{2,1},{1,0},{7,6},{6,5},{5,4},{11,10},{10,9},{9,8},{15,14},{... | collective-permute-start | bytes 1376264 | tf_op jit(solution)/shard_map/ppermute | solution.py:45
  168.0 58.6 %collective-permute-start.38 = (f16[2,112,1024]{2,1,0:T(8,128)(2,1)}, f16[2,112,1024]{2,1,0:T(8,128)(2,1)}, u32[]{:S(2)}, u32[]{:S(2)}) collective-permute-start(f16[2,112,1024]{2,1,0:T(8,128)(2,1)} %get-tuple-element.107), channel_id=1, source_target_pairs={{0,1},{1,2},{2,3},{4,5},{5,6},{6,7},{8,9},{9,10},{10,11},{12,13},{... | collective-permute-start | bytes 1376264 | tf_op jit(solution)/shard_map/ppermute | solution.py:44
  173.5 24.1 %collective-permute-start.11 = (f16[2,112,1024]{2,1,0:T(8,128)(2,1)S(1)}, f16[2,112,1024]{2,1,0:T(8,128)(2,1)S(1)}, u32[]{:S(2)}, u32[]{:S(2)}) collective-permute-start(f16[2,112,1024]{2,1,0:T(8,128)(2,1)S(1)} %get-tuple-element.78), channel_id=1, source_target_pairs={{0,1},{4,5},{8,9},{12,13},{16,17},{20,21},{24,25},{28,29}} | collective-permute-start | bytes 1376264 | tf_op jit(solution)/shard_map/ppermute | solution.py:44
  176.7 36.0 %collective-permute-start.20 = (f16[2,112,1024]{2,1,0:T(8,128)(2,1)}, f16[2,112,1024]{2,1,0:T(8,128)(2,1)}, u32[]{:S(2)}, u32[]{:S(2)}) collective-permute-start(f16[2,112,1024]{2,1,0:T(8,128)(2,1)} %get-tuple-element.88), channel_id=1, source_target_pairs={{3,2},{7,6},{11,10},{15,14},{19,18},{23,22},{27,26},{31,30}} | collective-permute-start | bytes 1376264 | tf_op jit(solution)/shard_map/ppermute | solution.py:45
  178.1 36.9 %collective-permute-start.28 = (f16[2,112,1024]{2,1,0:T(8,128)(2,1)}, f16[2,112,1024]{2,1,0:T(8,128)(2,1)}, u32[]{:S(2)}, u32[]{:S(2)}) collective-permute-start(f16[2,112,1024]{2,1,0:T(8,128)(2,1)} %get-tuple-element.99), channel_id=1, source_target_pairs={{0,1},{4,5},{8,9},{12,13},{16,17},{20,21},{24,25},{28,29}} | collective-permute-start | bytes 1376264 | tf_op jit(solution)/shard_map/ppermute | solution.py:44
  183.3 33.0 %collective-permute-start.29 = (f16[2,112,1024]{2,1,0:T(8,128)(2,1)}, f16[2,112,1024]{2,1,0:T(8,128)(2,1)}, u32[]{:S(2)}, u32[]{:S(2)}) collective-permute-start(f16[2,112,1024]{2,1,0:T(8,128)(2,1)} %get-tuple-element.100), channel_id=1, source_target_pairs={{3,2},{7,6},{11,10},{15,14},{19,18},{23,22},{27,26},{31,30}} | collective-permute-start | bytes 1376264 | tf_op jit(solution)/shard_map/ppermute | solution.py:45
  197.6 23.3 %collective-permute-start.12 = (f16[2,112,1024]{2,1,0:T(8,128)(2,1)}, f16[2,112,1024]{2,1,0:T(8,128)(2,1)}, u32[]{:S(2)}, u32[]{:S(2)}) collective-permute-start(f16[2,112,1024]{2,1,0:T(8,128)(2,1)} %get-tuple-element.80), channel_id=1, source_target_pairs={{0,1},{4,5},{8,9},{12,13},{16,17},{20,21},{24,25},{28,29}} | collective-permute-start | bytes 1376264 | tf_op jit(solution)/shard_map/ppermute | solution.py:44
  212.7 11.7 %collective-permute-start.13 = (f16[2,112,1024]{2,1,0:T(8,128)(2,1)}, f16[2,112,1024]{2,1,0:T(8,128)(2,1)S(1)}, u32[]{:S(2)}, u32[]{:S(2)}) collective-permute-start(f16[2,112,1024]{2,1,0:T(8,128)(2,1)} %get-tuple-element.81), channel_id=1, source_target_pairs={{3,2},{7,6},{11,10},{15,14},{19,18},{23,22},{27,26},{31,30}} | collective-permute-start | bytes 1376264 | tf_op jit(solution)/shard_map/ppermute | solution.py:45
  215.0 14.1 %collective-permute-start.39 = (f16[2,112,1024]{2,1,0:T(8,128)(2,1)}, f16[2,112,1024]{2,1,0:T(8,128)(2,1)S(1)}, u32[]{:S(2)}, u32[]{:S(2)}) collective-permute-start(f16[2,112,1024]{2,1,0:T(8,128)(2,1)} %get-tuple-element.108), channel_id=1, source_target_pairs={{3,2},{2,1},{1,0},{7,6},{6,5},{5,4},{11,10},{10,9},{9,8},{15,14},{... | collective-permute-start | bytes 1376264 | tf_op jit(solution)/shard_map/ppermute | solution.py:45
  216.3 15.8 %collective-permute-start.52 = (bf16[224,1024]{1,0:T(8,128)(2,1)}, bf16[224,1024]{1,0:T(8,128)(2,1)S(1)}, u32[]{:S(2)}, u32[]{:S(2)}) collective-permute-start(bf16[224,1024]{1,0:T(8,128)(2,1)} %pad_maximum_fusion.1), channel_id=1, source_target_pairs={{0,1},{1,2},{2,3},{4,5},{5,6},{6,7},{8,9},{9,10},{10,11},{12,13},{... | collective-permute-start | bytes 1376264 | tf_op jit(solution)/shard_map/ppermute | solution.py:58
  220.9 21.0 %collective-permute-start.21 = (f16[2,112,1024]{2,1,0:T(8,128)(2,1)S(1)}, f16[2,112,1024]{2,1,0:T(8,128)(2,1)S(1)}, u32[]{:S(2)}, u32[]{:S(2)}) collective-permute-start(f16[2,112,1024]{2,1,0:T(8,128)(2,1)S(1)} %get-tuple-element.89), channel_id=1, source_target_pairs={{0,1},{1,2},{4,5},{5,6},{8,9},{9,10},{12,13},{13,14},{16,17},{17,1... | collective-permute-start | bytes 1376264 | tf_op jit(solution)/shard_map/ppermute | solution.py:44
  224.4 19.4 %collective-permute-start.22 = (f16[2,112,1024]{2,1,0:T(8,128)(2,1)S(1)}, f16[2,112,1024]{2,1,0:T(8,128)(2,1)S(1)}, u32[]{:S(2)}, u32[]{:S(2)}) collective-permute-start(f16[2,112,1024]{2,1,0:T(8,128)(2,1)S(1)} %get-tuple-element.90), channel_id=1, source_target_pairs={{3,2},{2,1},{7,6},{6,5},{11,10},{10,9},{15,14},{14,13},{19,18},{18... | collective-permute-start | bytes 1376264 | tf_op jit(solution)/shard_map/ppermute | solution.py:45
  226.6 35.8 %collective-permute-start.30 = (f16[2,112,1024]{2,1,0:T(8,128)(2,1)S(1)}, f16[2,112,1024]{2,1,0:T(8,128)(2,1)S(1)}, u32[]{:S(2)}, u32[]{:S(2)}) collective-permute-start(f16[2,112,1024]{2,1,0:T(8,128)(2,1)S(1)} %get-tuple-element.101), channel_id=1, source_target_pairs={{0,1},{1,2},{4,5},{5,6},{8,9},{9,10},{12,13},{13,14},{16,17},{17,1... | collective-permute-start | bytes 1376264 | tf_op jit(solution)/shard_map/ppermute | solution.py:44
  229.1 34.0 %collective-permute-start.31 = (f16[2,112,1024]{2,1,0:T(8,128)(2,1)S(1)}, f16[2,112,1024]{2,1,0:T(8,128)(2,1)S(1)}, u32[]{:S(2)}, u32[]{:S(2)}) collective-permute-start(f16[2,112,1024]{2,1,0:T(8,128)(2,1)S(1)} %get-tuple-element.102), channel_id=1, source_target_pairs={{3,2},{2,1},{7,6},{6,5},{11,10},{10,9},{15,14},{14,13},{19,18},{18... | collective-permute-start | bytes 1376264 | tf_op jit(solution)/shard_map/ppermute | solution.py:45
  232.1 24.7 %collective-permute-start.14 = (f16[2,112,1024]{2,1,0:T(8,128)(2,1)S(1)}, f16[2,112,1024]{2,1,0:T(8,128)(2,1)S(1)}, u32[]{:S(2)}, u32[]{:S(2)}) collective-permute-start(f16[2,112,1024]{2,1,0:T(8,128)(2,1)S(1)} %get-tuple-element.82), channel_id=1, source_target_pairs={{0,1},{1,2},{4,5},{5,6},{8,9},{9,10},{12,13},{13,14},{16,17},{17,1... | collective-permute-start | bytes 1376264 | tf_op jit(solution)/shard_map/ppermute | solution.py:44
  241.9 19.4 %collective-permute-start.15 = (f16[2,112,1024]{2,1,0:T(8,128)(2,1)S(1)}, f16[2,112,1024]{2,1,0:T(8,128)(2,1)S(1)}, u32[]{:S(2)}, u32[]{:S(2)}) collective-permute-start(f16[2,112,1024]{2,1,0:T(8,128)(2,1)S(1)} %get-tuple-element.83), channel_id=1, source_target_pairs={{3,2},{2,1},{7,6},{6,5},{11,10},{10,9},{15,14},{14,13},{19,18},{18... | collective-permute-start | bytes 1376264 | tf_op jit(solution)/shard_map/ppermute | solution.py:45
  243.9 23.2 %collective-permute-start.55 = (bf16[224,1024]{1,0:T(8,128)(2,1)S(1)}, bf16[224,1024]{1,0:T(8,128)(2,1)S(1)}, u32[]{:S(2)}, u32[]{:S(2)}) collective-permute-start(bf16[224,1024]{1,0:T(8,128)(2,1)S(1)} %copy-done.15), channel_id=1, source_target_pairs={{1,0},{2,1},{3,2},{5,4},{6,5},{7,6},{9,8},{10,9},{11,10},{13,12},{... | collective-permute-start | bytes 1376264 | tf_op jit(solution)/shard_map/ppermute | solution.py:60
  256.9 15.3 %collective-permute-start.40 = (f16[2,112,1024]{2,1,0:T(8,128)(2,1)S(1)}, f16[2,112,1024]{2,1,0:T(8,128)(2,1)S(1)}, u32[]{:S(2)}, u32[]{:S(2)}) collective-permute-start(f16[2,112,1024]{2,1,0:T(8,128)(2,1)S(1)} %get-tuple-element.109), channel_id=1, source_target_pairs={{0,1},{4,5},{8,9},{12,13},{16,17},{20,21},{24,25},{28,29}} | collective-permute-start | bytes 1376264 | tf_op jit(solution)/shard_map/ppermute | solution.py:44
  261.3 15.3 %collective-permute-start.41 = (f16[2,112,1024]{2,1,0:T(8,128)(2,1)S(1)}, f16[2,112,1024]{2,1,0:T(8,128)(2,1)S(1)}, u32[]{:S(2)}, u32[]{:S(2)}) collective-permute-start(f16[2,112,1024]{2,1,0:T(8,128)(2,1)S(1)} %get-tuple-element.110), channel_id=1, source_target_pairs={{3,2},{7,6},{11,10},{15,14},{19,18},{23,22},{27,26},{31,30}} | collective-permute-start | bytes 1376264 | tf_op jit(solution)/shard_map/ppermute | solution.py:45
  262.4 26.6 %collective-permute-start.53 = (bf16[224,1024]{1,0:T(8,128)(2,1)S(1)}, bf16[224,1024]{1,0:T(8,128)(2,1)S(1)}, u32[]{:S(2)}, u32[]{:S(2)}) collective-permute-start(bf16[224,1024]{1,0:T(8,128)(2,1)S(1)} %collective-permute-done.52), channel_id=1, source_target_pairs={{1,2},{2,3},{5,6},{6,7},{9,10},{10,11},{13,14},{14,15},{17,18},{18... | collective-permute-start | bytes 1376264 | tf_op jit(solution)/shard_map/ppermute | solution.py:58
  263.2 18.6 %collective-permute-start.16 = (f16[2,112,1024]{2,1,0:T(8,128)(2,1)S(1)}, f16[2,112,1024]{2,1,0:T(8,128)(2,1)S(1)}, u32[]{:S(2)}, u32[]{:S(2)}) collective-permute-start(f16[2,112,1024]{2,1,0:T(8,128)(2,1)S(1)} %get-tuple-element.84), channel_id=1, source_target_pairs={{0,1},{1,2},{2,3},{4,5},{5,6},{6,7},{8,9},{9,10},{10,11},{12,13},{... | collective-permute-start | bytes 1376264 | tf_op jit(solution)/shard_map/ppermute | solution.py:44
  267.1 15.9 %collective-permute-start.17 = (f16[2,112,1024]{2,1,0:T(8,128)(2,1)S(1)}, f16[2,112,1024]{2,1,0:T(8,128)(2,1)S(1)}, u32[]{:S(2)}, u32[]{:S(2)}) collective-permute-start(f16[2,112,1024]{2,1,0:T(8,128)(2,1)S(1)} %get-tuple-element.85), channel_id=1, source_target_pairs={{3,2},{2,1},{1,0},{7,6},{6,5},{5,4},{11,10},{10,9},{9,8},{15,14},{... | collective-permute-start | bytes 1376264 | tf_op jit(solution)/shard_map/ppermute | solution.py:45
  272.2 19.0 %collective-permute-start.32 = (f16[2,112,1024]{2,1,0:T(8,128)(2,1)S(1)}, f16[2,112,1024]{2,1,0:T(8,128)(2,1)S(1)}, u32[]{:S(2)}, u32[]{:S(2)}) collective-permute-start(f16[2,112,1024]{2,1,0:T(8,128)(2,1)S(1)} %get-tuple-element.103), channel_id=1, source_target_pairs={{0,1},{1,2},{2,3},{4,5},{5,6},{6,7},{8,9},{9,10},{10,11},{12,13},{... | collective-permute-start | bytes 1376264 | tf_op jit(solution)/shard_map/ppermute | solution.py:44
  276.6 19.7 %collective-permute-start.33 = (f16[2,112,1024]{2,1,0:T(8,128)(2,1)S(1)}, f16[2,112,1024]{2,1,0:T(8,128)(2,1)S(1)}, u32[]{:S(2)}, u32[]{:S(2)}) collective-permute-start(f16[2,112,1024]{2,1,0:T(8,128)(2,1)S(1)} %get-tuple-element.104), channel_id=1, source_target_pairs={{3,2},{2,1},{1,0},{7,6},{6,5},{5,4},{11,10},{10,9},{9,8},{15,14},{... | collective-permute-start | bytes 1376264 | tf_op jit(solution)/shard_map/ppermute | solution.py:45
  281.8 20.2 %collective-permute-start.56 = (bf16[224,1024]{1,0:T(8,128)(2,1)S(1)}, bf16[224,1024]{1,0:T(8,128)(2,1)S(1)}, u32[]{:S(2)}, u32[]{:S(2)}) collective-permute-start(bf16[224,1024]{1,0:T(8,128)(2,1)S(1)} %collective-permute-done.55), channel_id=1, source_target_pairs={{1,0},{2,1},{5,4},{6,5},{9,8},{10,9},{13,12},{14,13},{17,16},{18,1... | collective-permute-start | bytes 1376264 | tf_op jit(solution)/shard_map/ppermute | solution.py:60
  283.1 61.8 %collective-permute-start.23 = (f16[2,112,1024]{2,1,0:T(8,128)(2,1)}, f16[2,112,1024]{2,1,0:T(8,128)(2,1)}, u32[]{:S(2)}, u32[]{:S(2)}) collective-permute-start(f16[2,112,1024]{2,1,0:T(8,128)(2,1)} %get-tuple-element.91), channel_id=1, source_target_pairs={{0,1},{1,2},{2,3},{4,5},{5,6},{6,7},{8,9},{9,10},{10,11},{12,13},{... | collective-permute-start | bytes 1376264 | tf_op jit(solution)/shard_map/ppermute | solution.py:44
  289.1 55.8 %collective-permute-start.24 = (f16[2,112,1024]{2,1,0:T(8,128)(2,1)S(1)}, f16[2,112,1024]{2,1,0:T(8,128)(2,1)}, u32[]{:S(2)}, u32[]{:S(2)}) collective-permute-start(f16[2,112,1024]{2,1,0:T(8,128)(2,1)S(1)} %get-tuple-element.92), channel_id=1, source_target_pairs={{3,2},{2,1},{1,0},{7,6},{6,5},{5,4},{11,10},{10,9},{9,8},{15,14},{... | collective-permute-start | bytes 1376264 | tf_op jit(solution)/shard_map/ppermute | solution.py:45
  291.2 29.0 %collective-permute-start.42 = (f16[2,112,1024]{2,1,0:T(8,128)(2,1)}, f16[2,112,1024]{2,1,0:T(8,128)(2,1)}, u32[]{:S(2)}, u32[]{:S(2)}) collective-permute-start(f16[2,112,1024]{2,1,0:T(8,128)(2,1)} %get-tuple-element.111), channel_id=1, source_target_pairs={{0,1},{1,2},{4,5},{5,6},{8,9},{9,10},{12,13},{13,14},{16,17},{17,1... | collective-permute-start | bytes 1376264 | tf_op jit(solution)/shard_map/ppermute | solution.py:44
  302.0 19.0 %collective-permute-start.43 = (f16[2,112,1024]{2,1,0:T(8,128)(2,1)}, f16[2,112,1024]{2,1,0:T(8,128)(2,1)}, u32[]{:S(2)}, u32[]{:S(2)}) collective-permute-start(f16[2,112,1024]{2,1,0:T(8,128)(2,1)} %get-tuple-element.112), channel_id=1, source_target_pairs={{3,2},{2,1},{7,6},{6,5},{11,10},{10,9},{15,14},{14,13},{19,18},{18... | collective-permute-start | bytes 1376264 | tf_op jit(solution)/shard_map/ppermute | solution.py:45
  313.9 28.2 %collective-permute-start.18 = (f16[2,112,1024]{2,1,0:T(8,128)(2,1)}, f16[2,112,1024]{2,1,0:T(8,128)(2,1)}, u32[]{:S(2)}, u32[]{:S(2)}) collective-permute-start(f16[2,112,1024]{2,1,0:T(8,128)(2,1)} %get-tuple-element.86), channel_id=1, source_target_pairs={{0,1},{4,5},{8,9},{12,13},{16,17},{20,21},{24,25},{28,29}} | collective-permute-start | bytes 1376264 | tf_op jit(solution)/shard_map/ppermute | solution.py:44
  317.6 145.9 %all-gather.11.cloned.1.call-start = ((), (), s32[]{:S(2)}) async-start(), calls=%async_computation.3 | async-start | bytes 5505024 | tf_op jit(solution)/shard_map/all_gather | solution.py:115
  320.2 23.2 %collective-permute-start.19 = (f16[2,112,1024]{2,1,0:T(8,128)(2,1)S(1)}, f16[2,112,1024]{2,1,0:T(8,128)(2,1)S(1)}, u32[]{:S(2)}, u32[]{:S(2)}) collective-permute-start(f16[2,112,1024]{2,1,0:T(8,128)(2,1)S(1)} %copy-done.16), channel_id=1, source_target_pairs={{3,2},{7,6},{11,10},{15,14},{19,18},{23,22},{27,26},{31,30}} | collective-permute-start | bytes 1376264 | tf_op jit(solution)/shard_map/ppermute | solution.py:45
  324.6 20.3 %collective-permute-start.58 = (bf16[224,1024]{1,0:T(8,128)(2,1)S(1)}, bf16[224,1024]{1,0:T(8,128)(2,1)S(1)}, u32[]{:S(2)}, u32[]{:S(2)}) collective-permute-start(bf16[224,1024]{1,0:T(8,128)(2,1)S(1)} %pad_maximum_fusion.2), channel_id=1, source_target_pairs={{0,1},{1,2},{2,3},{4,5},{5,6},{6,7},{8,9},{9,10},{10,11},{12,13},{... | collective-permute-start | bytes 1376264 | tf_op jit(solution)/shard_map/ppermute | solution.py:58
  342.1 14.7 %collective-permute-start.61 = (bf16[224,1024]{1,0:T(8,128)(2,1)S(1)}, bf16[224,1024]{1,0:T(8,128)(2,1)S(1)}, u32[]{:S(2)}, u32[]{:S(2)}) collective-permute-start(bf16[224,1024]{1,0:T(8,128)(2,1)S(1)} %pad_maximum_fusion.2), channel_id=1, source_target_pairs={{1,0},{2,1},{3,2},{5,4},{6,5},{7,6},{9,8},{10,9},{11,10},{13,12},{... | collective-permute-start | bytes 1376264 | tf_op jit(solution)/shard_map/ppermute | solution.py:60
  344.9 13.4 %collective-permute-start.59 = (bf16[224,1024]{1,0:T(8,128)(2,1)S(1)}, bf16[224,1024]{1,0:T(8,128)(2,1)S(1)}, u32[]{:S(2)}, u32[]{:S(2)}) collective-permute-start(bf16[224,1024]{1,0:T(8,128)(2,1)S(1)} %collective-permute-done.58), channel_id=1, source_target_pairs={{1,2},{2,3},{5,6},{6,7},{9,10},{10,11},{13,14},{14,15},{17,18},{18... | collective-permute-start | bytes 1376264 | tf_op jit(solution)/shard_map/ppermute | solution.py:58
  347.4 16.8 %collective-permute-start.44 = (f16[2,112,1024]{2,1,0:T(8,128)(2,1)S(1)}, f16[2,112,1024]{2,1,0:T(8,128)(2,1)S(1)}, u32[]{:S(2)}, u32[]{:S(2)}) collective-permute-start(f16[2,112,1024]{2,1,0:T(8,128)(2,1)S(1)} %get-tuple-element.113), channel_id=1, source_target_pairs={{0,1},{1,2},{4,5},{5,6},{8,9},{9,10},{12,13},{13,14},{16,17},{17,1... | collective-permute-start | bytes 1376264 | tf_op jit(solution)/shard_map/ppermute | solution.py:44
  356.7 22.2 %collective-permute-start.62 = (bf16[224,1024]{1,0:T(8,128)(2,1)S(1)}, bf16[224,1024]{1,0:T(8,128)(2,1)S(1)}, u32[]{:S(2)}, u32[]{:S(2)}) collective-permute-start(bf16[224,1024]{1,0:T(8,128)(2,1)S(1)} %collective-permute-done.61), channel_id=1, source_target_pairs={{1,0},{2,1},{5,4},{6,5},{9,8},{10,9},{13,12},{14,13},{17,16},{18,1... | collective-permute-start | bytes 1376264 | tf_op jit(solution)/shard_map/ppermute | solution.py:60
  358.2 22.0 %collective-permute-start.60 = (bf16[224,1024]{1,0:T(8,128)(2,1)S(1)}, bf16[224,1024]{1,0:T(8,128)(2,1)S(1)}, u32[]{:S(2)}, u32[]{:S(2)}) collective-permute-start(bf16[224,1024]{1,0:T(8,128)(2,1)S(1)} %collective-permute-done.59), channel_id=1, source_target_pairs={{2,3},{6,7},{10,11},{14,15},{18,19},{22,23},{26,27},{30,31}} | collective-permute-start | bytes 1376264 | tf_op jit(solution)/shard_map/ppermute | solution.py:58
  359.1 42.9 %collective-permute-start.25 = (bf16[112,1024]{1,0:T(8,128)(2,1)S(1)}, bf16[112,1024]{1,0:T(8,128)(2,1)}, u32[]{:S(2)}, u32[]{:S(2)}) collective-permute-start(bf16[112,1024]{1,0:T(8,128)(2,1)S(1)} %multiply_convert_fusion.7), channel_id=1, source_target_pairs={{0,0},{1,4},{2,8},{3,12},{4,1},{5,5},{6,9},{7,13},{8,2},{9,6},{10,... | collective-permute-start | bytes 688136 | tf_op jit(solution)/shard_map/ppermute | solution.py:122
  364.2 48.9 %collective-permute-start.46 = (f16[2,112,1024]{2,1,0:T(8,128)(2,1)}, f16[2,112,1024]{2,1,0:T(8,128)(2,1)}, u32[]{:S(2)}, u32[]{:S(2)}) collective-permute-start(f16[2,112,1024]{2,1,0:T(8,128)(2,1)} %get-tuple-element.117), channel_id=1, source_target_pairs={{0,1},{1,2},{2,3},{4,5},{5,6},{6,7},{8,9},{9,10},{10,11},{12,13},{... | collective-permute-start | bytes 1376264 | tf_op jit(solution)/shard_map/ppermute | solution.py:44
  377.6 35.5 %collective-permute-start.47 = (f16[2,112,1024]{2,1,0:T(8,128)(2,1)}, f16[2,112,1024]{2,1,0:T(8,128)(2,1)}, u32[]{:S(2)}, u32[]{:S(2)}) collective-permute-start(f16[2,112,1024]{2,1,0:T(8,128)(2,1)} %get-tuple-element.118), channel_id=1, source_target_pairs={{3,2},{2,1},{1,0},{7,6},{6,5},{5,4},{11,10},{10,9},{9,8},{15,14},{... | collective-permute-start | bytes 1376264 | tf_op jit(solution)/shard_map/ppermute | solution.py:45
  378.9 21.6 %collective-permute-start.63 = (bf16[224,1024]{1,0:T(8,128)(2,1)S(1)}, bf16[224,1024]{1,0:T(8,128)(2,1)S(1)}, u32[]{:S(2)}, u32[]{:S(2)}) collective-permute-start(bf16[224,1024]{1,0:T(8,128)(2,1)S(1)} %collective-permute-done.62), channel_id=1, source_target_pairs={{1,0},{5,4},{9,8},{13,12},{17,16},{21,20},{25,24},{29,28}} | collective-permute-start | bytes 1376264 | tf_op jit(solution)/shard_map/ppermute | solution.py:60
  413.2 12.3 %collective-permute-start.49 = (f16[2,112,1024]{2,1,0:T(8,128)(2,1)S(1)}, f16[2,112,1024]{2,1,0:T(8,128)(2,1)S(1)}, u32[]{:S(2)}, u32[]{:S(2)}) collective-permute-start(f16[2,112,1024]{2,1,0:T(8,128)(2,1)S(1)} %get-tuple-element.121), channel_id=1, source_target_pairs={{0,1},{1,2},{2,3},{4,5},{5,6},{6,7},{8,9},{9,10},{10,11},{12,13},{... | collective-permute-start | bytes 1376264 | tf_op jit(solution)/shard_map/ppermute | solution.py:44
  414.7 16.9 %collective-permute-start.50 = (f16[2,112,1024]{2,1,0:T(8,128)(2,1)S(1)}, f16[2,112,1024]{2,1,0:T(8,128)(2,1)S(1)}, u32[]{:S(2)}, u32[]{:S(2)}) collective-permute-start(f16[2,112,1024]{2,1,0:T(8,128)(2,1)S(1)} %get-tuple-element.122), channel_id=1, source_target_pairs={{3,2},{2,1},{1,0},{7,6},{6,5},{5,4},{11,10},{10,9},{9,8},{15,14},{... | collective-permute-start | bytes 1376264 | tf_op jit(solution)/shard_map/ppermute | solution.py:45
  418.1 15.0 %collective-permute-start.48 = (bf16[112,1024]{1,0:T(8,128)(2,1)S(1)}, bf16[112,1024]{1,0:T(8,128)(2,1)S(1)}, u32[]{:S(2)}, u32[]{:S(2)}) collective-permute-start(bf16[112,1024]{1,0:T(8,128)(2,1)S(1)} %multiply_convert_fusion.5), channel_id=1, source_target_pairs={{0,0},{1,4},{2,8},{3,12},{4,1},{5,5},{6,9},{7,13},{8,2},{9,6},{10,... | collective-permute-start | bytes 688136 | tf_op jit(solution)/shard_map/ppermute | solution.py:122
  432.5 20.9 %collective-permute-start.51 = (bf16[112,1024]{1,0:T(8,128)(2,1)S(1)}, bf16[112,1024]{1,0:T(8,128)(2,1)S(1)}, u32[]{:S(2)}, u32[]{:S(2)}) collective-permute-start(bf16[112,1024]{1,0:T(8,128)(2,1)S(1)} %multiply_convert_fusion.4), channel_id=1, source_target_pairs={{0,0},{1,4},{2,8},{3,12},{4,1},{5,5},{6,9},{7,13},{8,2},{9,6},{10,... | collective-permute-start | bytes 688136 | tf_op jit(solution)/shard_map/ppermute | solution.py:122
  (27 other events, 525.3 us)
Sparse Core Ops, SparseCore 0:
  9.2 39.4 all-gather.6
  50.6 36.7 all-gather.4
  317.7 48.0 all-gather.8
  402.1 48.4 all-gather.10

commit v3 on v2

--- a/solution.py
+++ b/solution.py
@@ -6,8 +6,8 @@
 from jax.sharding import PartitionSpec as P
 
 HALVES = 2
-PIECES = 2
-WINDOW = 4
+PIECES = 1
+WINDOW = 3
 CARRY = jnp.float16
 
 

time: 506 us -> 511 us (level)
  waiting for transfers between devices: 120 us -> 244 us
  starting transfers between devices: 155 us -> 89.1 us
  blocking collectives: 52.6 us -> 0 us
    all_gather x0 -> x2, waiting for transfers between devices: none -> 55.9 us  [local(): norm = lax.all_gather(norm, 'col', axis=0, tiled=True)]
    all_gather x4 -> x0, blocking collectives: 52.6 us -> none  [local(): norm = lax.all_gather(norm, 'col', axis=0, tiled=True)]
    ppermute x24 -> x12, starting transfers between devices: 104 us -> 51.8 us  [reduce_to_owners(): lax.ppermute(rise, 'tok', [(i, i + 1) for i in range(step)])]
    ppermute x24 -> x12, waiting for transfers between devices: 48.3 us -> 94.6 us  [reduce_to_owners(): lax.ppermute(rise, 'tok', [(i, i + 1) for i in range(step)])]
    all_gather x2, waiting for transfers between devices: 0.01 us -> 10 us  [local(): norm = lax.all_gather(norm, 'row', axis=0, tiled=True)]
    ppermute x24 -> x12, starting transfers between devices: 26.9 us -> 17.8 us  [reduce_to_owners(): lax.ppermute(fall, 'tok', [(depth - 1 - i, depth - 2 - i) for i in range(...]
    ppermute x6, waiting for transfers between devices: 2.3 us -> 10.9 us  [gather_line(): lax.ppermute(ups[-1], 'tok', [(i, i + 1) for i in range(step - 1, depth -...]
    slice x4 -> x0, local copies, waits for them, and re-layouts: 7.94 us -> none  [the longest x2 5.71 us: partial_sums(): return [part[:, :, q] for q in range(PIECES)]]
  transfers between devices with their start and end apart: 68 -> 44, of which waited for: 15 -> 23; matrix products, arithmetic and copies ran while one was open for 25% -> 24% of each run, Pallas kernels for 0% -> 0%
where the time goes in v3:
time: 511 us; the launch traced here: 502 us
  waiting for transfers between devices  244 us (48%)
  starting transfers between devices  89.1 us (17%)
  matrix products  67.5 us (13%)
  other arithmetic  44.9 us (9%)
  local copies, waits for them, and re-layouts  41.7 us (8%)
  between operations  14.5 us (3%)
    ppermute x12, waiting for transfers between devices, reduce_to_owners(): lax.ppermute(rise, 'tok', [(i, i + 1) for i in range(step)])  94.6 us
    all_gather x2, waiting for transfers between devices, local(): norm = lax.all_gather(norm, 'col', axis=0, tiled=True)  55.9 us
    ppermute x12, starting transfers between devices, reduce_to_owners(): lax.ppermute(rise, 'tok', [(i, i + 1) for i in range(step)])  51.8 us
    dot_general x4, matrix products, partial_sums(): lax.dot_general(weights, full, (((0,), (1,)), ((), ())), preferred_elemen...  45.7 us
    ppermute x6, waiting for transfers between devices, gather_line(): lax.ppermute(downs[-1], 'tok', [(i + 1, i) for i in range(depth - step)])  35.3 us
    all_gather x1, waiting for transfers between devices, local(): lax.all_gather(second_inputs, ('row', 'col'), axis=0, tiled=True)  27.8 us
    convert_element_type x8, other arithmetic, reduce_to_owners(): rise, fall = (rise.astype(CARRY), fall.astype(CARRY))  27.2 us
    slice x2, local copies, waits for them, and re-layouts, partial_sums(): weights = weights[:, :, half * size:(half + 1) * size]  24.4 us
  transfers between devices with their start and end apart: 44, of which 23 were waited for; matrix products, arithmetic and copies ran while one was open for 24% of the time, Pallas kernels for 0%

profile of v3, /device:TPU:0, one launch (start us, length us, event | category | flops | bytes accessed | tf_op | source)
XLA Modules:
  0.0 502.1 jit_solution(3737792015418940020)
XLA Ops:
  8.1 12.8 %fusion.68 = (bf16[2048,2,896]{2,1,0:T(2,128)(2,1)}, bf16[2048,2,896]{2,1,0:T(2,128)(2,1)}) fusion(bf16[2048,2,1792]{2,1,0:T(2,128)(2,1)} %param.7), kind=kLoop, calls=%fused_computation.118 | loop fusion | bytes 29360128 | tf_op jit(solution)/shard_map/slice | solution.py:81
  20.9 27.8 %all-gather.9.cloned.1.call-done = bf16[1024,2048]{1,0:T(8,128)(2,1)} async-done(((bf16[128,2048]{1,0:T(8,128)(2,1)}), bf16[1024,2048]{1,0:T(8,128)(2,1)}) %all-gather.9.cloned.1.call-update) | async-done | bytes 4194320 | tf_op jit(solution)/shard_map/all_gather | solution.py:98
  48.7 11.8 %fusion.15 = f16[2,896,1024]{2,1,0:T(8,128)(2,1)S(1)} fusion(bf16[1024,2048]{1,0:T(8,128)(2,1)} %all-gather.9.cloned.1.call-done, bf16[2048,2,896]{2,1,0:T(2,128)(2,1)} %get-tuple-element.75), kind=kOutput, calls=%fused_computation.17 | convolution fusion | flops 7518027776 | bytes 15204352 | tf_op jit(solution)/shard_map/dot_general | solution.py:84
  60.5 1.8 dynamic-slice_bitcast_fusion.3
  62.3 3.4 collective-permute-start
  65.8 1.6 collective-permute-start.3
  67.4 18.3 %collective-permute-done = f16[2,224,1024]{2,1,0:T(8,128)(2,1)S(1)} collective-permute-done((f16[2,224,1024]{2,1,0:T(8,128)(2,1)S(1)}, f16[2,224,1024]{2,1,0:T(8,128)(2,1)S(1)}, u32[]{:S(2)}, u32[]{:S(2)}) %collective-permute-start) | collective-permute-done | bytes 917536 | tf_op jit(solution)/shard_map/ppermute | solution.py:44
  86.7 11.9 %fusion.20 = f16[1024,2,896]{0,2,1:T(8,128)(2,1)S(1)} fusion(bf16[2048,2,896]{2,1,0:T(2,128)(2,1)} %get-tuple-element.76, bf16[1024,2048]{1,0:T(8,128)(2,1)} %all-gather.9.cloned.1.call-done), kind=kOutput, calls=%fused_computation.18 | convolution fusion | flops 7518027776 | bytes 15204352 | tf_op jit(solution)/shard_map/dot_general | solution.py:84
  98.7 1.8 copy-done.5
  100.5 1.8 dynamic-slice_bitcast_fusion
  102.2 4.8 collective-permute-start.1
  107.1 11.6 %fusion.69 = (bf16[2048,2,896]{2,1,0:T(2,128)(2,1)}, bf16[2048,2,896]{2,1,0:T(2,128)(2,1)}) fusion(bf16[2048,2,1792]{2,1,0:T(2,128)(2,1)S(1)} %bitcast.189), kind=kLoop, calls=%fused_computation.119 | loop fusion | bytes 29360128 | tf_op jit(solution)/shard_map/slice | solution.py:81
  118.7 4.0 fusion.50
  124.8 1.6 collective-permute-start.7
  127.8 11.9 %fusion.25 = f16[1024,2,896]{0,2,1:T(8,128)(2,1)S(1)} fusion(bf16[2048,2,896]{2,1,0:T(2,128)(2,1)} %get-tuple-element.77, bf16[1024,2048]{1,0:T(8,128)(2,1)} %all-gather.7.cloned.1.call-done), kind=kOutput, calls=%fused_computation.19 | convolution fusion | flops 7518027776 | bytes 15204352 | tf_op jit(solution)/shard_map/dot_general | solution.py:84
  140.4 5.5 %collective-permute-done.2 = f16[2,224,1024]{2,1,0:T(8,128)(2,1)S(1)} collective-permute-done((f16[2,224,1024]{2,1,0:T(8,128)(2,1)}, f16[2,224,1024]{2,1,0:T(8,128)(2,1)S(1)}, u32[]{:S(2)}, u32[]{:S(2)}) %collective-permute-start.2) | collective-permute-done | bytes 917536 | tf_op jit(solution)/shard_map/ppermute | solution.py:44
  145.9 4.3 collective-permute-start.5
  150.2 1.7 collective-permute-start.6
  151.9 3.4 fusion.47
  156.6 2.1 collective-permute-start.9
  158.7 12.3 %collective-permute-done.5 = f16[2,224,1024]{2,1,0:T(8,128)(2,1)S(1)} collective-permute-done((f16[2,224,1024]{2,1,0:T(8,128)(2,1)S(1)}, f16[2,224,1024]{2,1,0:T(8,128)(2,1)S(1)}, u32[]{:S(2)}, u32[]{:S(2)}) %collective-permute-start.5) | collective-permute-done | bytes 917536 | tf_op jit(solution)/shard_map/ppermute | solution.py:44
  171.0 10.0 %fusion.30 = f16[1024,2,896]{0,2,1:T(8,128)(2,1)S(1)} fusion(bf16[2048,2,896]{2,1,0:T(2,128)(2,1)S(1)} %bitcast.207, bf16[1024,2048]{1,0:T(8,128)(2,1)} %all-gather.7.cloned.1.call-done), kind=kOutput, calls=%fused_computation.20 | convolution fusion | flops 7518027776 | bytes 15204352 | tf_op jit(solution)/shard_map/dot_general | solution.py:84
  181.0 1.8 copy-done.2
  182.8 1.8 dynamic-slice_bitcast_fusion.1
  184.6 5.3 %collective-permute-start.15 = (f16[2,224,1024]{2,1,0:T(8,128)(2,1)}, f16[2,224,1024]{2,1,0:T(8,128)(2,1)}, u32[]{:S(2)}, u32[]{:S(2)}) collective-permute-start(f16[2,224,1024]{2,1,0:T(8,128)(2,1)} %get-tuple-element.49), channel_id=1, source_target_pairs={{0,1},{4,5},{8,9},{12,13},{16,17},{20,21},{24,25},{28,29}} | collective-permute-start | bytes 2752520 | tf_op jit(solution)/shard_map/ppermute | solution.py:44
  190.0 1.6 collective-permute-start.16
  191.6 2.6 fusion.37
  194.2 1.6 collective-permute-start.19
  197.1 3.4 fusion.49
  200.5 9.9 %collective-permute-done.15 = f16[2,224,1024]{2,1,0:T(8,128)(2,1)} collective-permute-done((f16[2,224,1024]{2,1,0:T(8,128)(2,1)}, f16[2,224,1024]{2,1,0:T(8,128)(2,1)}, u32[]{:S(2)}, u32[]{:S(2)}) %collective-permute-start.15) | collective-permute-done | bytes 917536 | tf_op jit(solution)/shard_map/ppermute | solution.py:44
  210.4 3.6 fusion.42
  214.0 5.4 %collective-permute-start.17 = (f16[2,224,1024]{2,1,0:T(8,128)(2,1)}, f16[2,224,1024]{2,1,0:T(8,128)(2,1)}, u32[]{:S(2)}, u32[]{:S(2)}) collective-permute-start(f16[2,224,1024]{2,1,0:T(8,128)(2,1)} %get-tuple-element.51), channel_id=1, source_target_pairs={{0,1},{1,2},{4,5},{5,6},{8,9},{9,10},{12,13},{13,14},{16,17},{17,1... | collective-permute-start | bytes 2752520 | tf_op jit(solution)/shard_map/ppermute | solution.py:44
  221.0 3.4 fusion.39
  224.4 5.5 %collective-permute-done.19 = f16[2,224,1024]{2,1,0:T(8,128)(2,1)S(1)} collective-permute-done((f16[2,224,1024]{2,1,0:T(8,128)(2,1)S(1)}, f16[2,224,1024]{2,1,0:T(8,128)(2,1)S(1)}, u32[]{:S(2)}, u32[]{:S(2)}) %collective-permute-start.19) | collective-permute-done | bytes 917536 | tf_op jit(solution)/shard_map/ppermute | solution.py:44
  230.0 4.4 collective-permute-start.21
  235.9 2.0 fusion.36
  237.9 11.9 %collective-permute-done.17 = f16[2,224,1024]{2,1,0:T(8,128)(2,1)} collective-permute-done((f16[2,224,1024]{2,1,0:T(8,128)(2,1)}, f16[2,224,1024]{2,1,0:T(8,128)(2,1)}, u32[]{:S(2)}, u32[]{:S(2)}) %collective-permute-start.17) | collective-permute-done | bytes 917536 | tf_op jit(solution)/shard_map/ppermute | solution.py:44
  249.7 3.7 fusion.41
  253.4 13.5 %collective-permute-done.21 = f16[2,224,1024]{2,1,0:T(8,128)(2,1)S(1)} collective-permute-done((f16[2,224,1024]{2,1,0:T(8,128)(2,1)}, f16[2,224,1024]{2,1,0:T(8,128)(2,1)S(1)}, u32[]{:S(2)}, u32[]{:S(2)}) %collective-permute-start.21) | collective-permute-done | bytes 917536 | tf_op jit(solution)/shard_map/ppermute | solution.py:44
  266.9 2.1 fusion.35
  270.0 4.3 collective-permute-start.26
  275.6 6.2 %collective-permute-done.26 = bf16[224,1024]{1,0:T(8,128)(2,1)S(1)} collective-permute-done((bf16[224,1024]{1,0:T(8,128)(2,1)S(1)}, bf16[224,1024]{1,0:T(8,128)(2,1)S(1)}, u32[]{:S(2)}, u32[]{:S(2)}) %collective-permute-start.26) | collective-permute-done | bytes 458784 | tf_op jit(solution)/shard_map/ppermute | solution.py:58
  283.2 2.7 collective-permute-done.29
  288.7 8.0 %collective-permute-done.30 = bf16[224,1024]{1,0:T(8,128)(2,1)S(1)} collective-permute-done((bf16[224,1024]{1,0:T(8,128)(2,1)S(1)}, bf16[224,1024]{1,0:T(8,128)(2,1)S(1)}, u32[]{:S(2)}, u32[]{:S(2)}) %collective-permute-start.30) | collective-permute-done | bytes 458784 | tf_op jit(solution)/shard_map/ppermute | solution.py:60
  300.4 6.7 %collective-permute-done.31 = bf16[224,1024]{1,0:T(8,128)(2,1)S(1)} collective-permute-done((bf16[224,1024]{1,0:T(8,128)(2,1)S(1)}, bf16[224,1024]{1,0:T(8,128)(2,1)S(1)}, u32[]{:S(2)}, u32[]{:S(2)}) %collective-permute-start.31) | collective-permute-done | bytes 458784 | tf_op jit(solution)/shard_map/ppermute | solution.py:60
  311.9 4.7 collective-permute-done.32
  317.2 4.9 collective-permute-done.35
  324.2 8.4 %collective-permute-start.10 = (f16[2,224,1024]{2,1,0:T(8,128)(2,1)S(1)}, f16[2,224,1024]{2,1,0:T(8,128)(2,1)}, u32[]{:S(2)}, u32[]{:S(2)}) collective-permute-start(f16[2,224,1024]{2,1,0:T(8,128)(2,1)S(1)} %copy-done.10), channel_id=1, source_target_pairs={{0,1},{1,2},{4,5},{5,6},{8,9},{9,10},{12,13},{13,14},{16,17},{17,1... | collective-permute-start | bytes 2752520 | tf_op jit(solution)/shard_map/ppermute | solution.py:44
  332.6 1.6 collective-permute-start.11
  335.9 13.0 %collective-permute-done.37 = bf16[224,1024]{1,0:T(8,128)(2,1)S(1)} collective-permute-done((bf16[224,1024]{1,0:T(8,128)(2,1)S(1)}, bf16[224,1024]{1,0:T(8,128)(2,1)S(1)}, u32[]{:S(2)}, u32[]{:S(2)}) %collective-permute-start.37) | collective-permute-done | bytes 458784 | tf_op jit(solution)/shard_map/ppermute | solution.py:60
  350.4 3.1 fusion.46
  353.5 6.8 %collective-permute-start.12 = (f16[2,224,1024]{2,1,0:T(8,128)(2,1)S(1)}, f16[2,224,1024]{2,1,0:T(8,128)(2,1)S(1)}, u32[]{:S(2)}, u32[]{:S(2)}) collective-permute-start(f16[2,224,1024]{2,1,0:T(8,128)(2,1)S(1)} %get-tuple-element.47), channel_id=1, source_target_pairs={{0,1},{1,2},{2,3},{4,5},{5,6},{6,7},{8,9},{9,10},{10,11},{12,13},{... | collective-permute-start | bytes 2752520 | tf_op jit(solution)/shard_map/ppermute | solution.py:44
  361.6 4.6 collective-permute-start.23
  367.5 12.4 %collective-permute-done.12 = f16[2,224,1024]{2,1,0:T(8,128)(2,1)S(1)} collective-permute-done((f16[2,224,1024]{2,1,0:T(8,128)(2,1)S(1)}, f16[2,224,1024]{2,1,0:T(8,128)(2,1)S(1)}, u32[]{:S(2)}, u32[]{:S(2)}) %collective-permute-start.12) | collective-permute-done | bytes 917536 | tf_op jit(solution)/shard_map/ppermute | solution.py:44
  379.9 4.2 collective-permute-done.13
  384.1 1.8 fusion.54
  385.9 3.9 collective-permute-done.23
  389.7 4.2 collective-permute-done.24
  393.9 1.8 fusion.45
  400.5 10.0 %all-gather.17.cloned.1.call-done = bf16[1792,1024]{1,0:T(8,128)(2,1)} async-done(((bf16[896,1024]{1,0:T(8,128)(2,1)}), bf16[1792,1024]{1,0:T(8,128)(2,1)}) %all-gather.17.cloned.1.call-update) | async-done | bytes 3670032 | tf_op jit(solution)/shard_map/all_gather | solution.py:115
  410.4 6.9 %pad_maximum_fusion = bf16[2,1792,1024]{2,1,0:T(8,128)(2,1)} fusion(bf16[2,896,1024]{2,1,0:T(8,128)(2,1)} %bitcast.210, bf16[2,896,1024]{2,1,0:T(8,128)(2,1)} %bitcast.209), kind=kLoop, calls=%fused_computation.1 | loop fusion | flops 14680064 | bytes 14680064 | tf_op jit(solution)/shard_map/concatenate | solution.py:117
  417.4 28.5 %all-gather.11.cloned.1.call-done = bf16[896,1024]{1,0:T(8,128)(2,1)} async-done(((bf16[224,1024]{1,0:T(8,128)(2,1)}), bf16[896,1024]{1,0:T(8,128)(2,1)}) %all-gather.11.cloned.1.call-update) | async-done | bytes 1835024 | tf_op jit(solution)/shard_map/all_gather | solution.py:123
  445.8 27.4 %all-gather.13.cloned.1.call-done = bf16[896,1024]{1,0:T(8,128)(2,1)} async-done(((bf16[224,1024]{1,0:T(8,128)(2,1)}), bf16[896,1024]{1,0:T(8,128)(2,1)}) %all-gather.13.cloned.1.call-update) | async-done | bytes 1835024 | tf_op jit(solution)/shard_map/all_gather | solution.py:123
  473.2 21.8 %convolution_multiply_fusion = f32[1792,3584]{1,0:T(8,128)} fusion(bf16[3584,1024]{1,0:T(8,128)(2,1)} %bitcast.208, bf16[896,1024]{1,0:T(8,128)(2,1)} %all-gather.13.cloned.1.call-done, bf16[896,1024]{1,0:T(8,128)(2,1)} %all-gather.11.cloned.1.call-done), kind=kOutput, calls=%fused_computation | convolution fusion | flops 13167099904 | bytes 36700160 | tf_op jit(solution)/shard_map/dot_general | solution.py:134
  (140 shorter events, 40.1 us)
Async XLA Ops:
  6.5 42.2 %all-gather.9.cloned.1.call-start = ((), (), s32[]{:S(2)}) async-start(), calls=%async_computation.1 | async-start | bytes 4718592 | tf_op jit(solution)/shard_map/all_gather | solution.py:98
  7.3 119.1 %all-gather.7.cloned.1.call-start = ((), (), s32[]{:S(2)}) async-start(), calls=%async_computation | async-start | bytes 4718592 | tf_op jit(solution)/shard_map/all_gather | solution.py:99
  8.0 392.5 %all-gather.15.cloned.1.call-start = ((), (), s32[]{:S(2)}) async-start(), calls=%async_computation.4 | async-start | bytes 5505024 | tf_op jit(solution)/shard_map/all_gather | solution.py:115
  60.5 25.2 %copy-start.8 = (f16[2,896,1024]{2,1,0:T(8,128)(2,1)}, f16[2,896,1024]{2,1,0:T(8,128)(2,1)S(1)}, u32[]{:S(2)}) copy-start(f16[2,896,1024]{2,1,0:T(8,128)(2,1)S(1)} %fusion.15) | copy-start | bytes 11010052
  62.3 23.4 %collective-permute-start = (f16[2,224,1024]{2,1,0:T(8,128)(2,1)S(1)}, f16[2,224,1024]{2,1,0:T(8,128)(2,1)S(1)}, u32[]{:S(2)}, u32[]{:S(2)}) collective-permute-start(f16[2,224,1024]{2,1,0:T(8,128)(2,1)S(1)} %get-tuple-element.100), channel_id=1, source_target_pairs={{0,1},{4,5},{8,9},{12,13},{16,17},{20,21},{24,25},{28,29}} | collective-permute-start | bytes 2752520 | tf_op jit(solution)/shard_map/ppermute | solution.py:44
  65.8 52.9 %collective-permute-start.3 = (f16[2,224,1024]{2,1,0:T(8,128)(2,1)}, f16[2,224,1024]{2,1,0:T(8,128)(2,1)}, u32[]{:S(2)}, u32[]{:S(2)}) collective-permute-start(f16[2,224,1024]{2,1,0:T(8,128)(2,1)} %get-tuple-element.99), channel_id=1, source_target_pairs={{3,2},{7,6},{11,10},{15,14},{19,18},{23,22},{27,26},{31,30}} | collective-permute-start | bytes 2752520 | tf_op jit(solution)/shard_map/ppermute | solution.py:45
  86.7 20.3 %slice-start = ((s8[14680064]{0:T(1024)(128)(4,1)}), s8[4194304]{0:T(1024)(128)(4,1)S(1)}, s32[]{:S(2)}) async-start(s8[14680064]{0:T(1024)(128)(4,1)} %bitcast.188), calls=%async_computation.6 | async-start | bytes 8388608
  86.7 20.3 %slice-start.1 = ((s8[14680064]{0:T(1024)(128)(4,1)}), s8[4194304]{0:T(1024)(128)(4,1)S(1)}, s32[]{:S(2)}) async-start(s8[14680064]{0:T(1024)(128)(4,1)} %bitcast.188), calls=%async_computation.7 | async-start | bytes 8388608
  86.7 20.3 %slice-start.2 = ((s8[14680064]{0:T(1024)(128)(4,1)}), s8[4194304]{0:T(1024)(128)(4,1)S(1)}, s32[]{:S(2)}) async-start(s8[14680064]{0:T(1024)(128)(4,1)} %bitcast.188), calls=%async_computation.8 | async-start | bytes 8388608
  86.7 20.4 %slice-start.3 = ((s8[14680064]{0:T(1024)(128)(4,1)}), s8[2097152]{0:T(1024)(128)(4,1)S(1)}, s32[]{:S(2)}) async-start(s8[14680064]{0:T(1024)(128)(4,1)} %bitcast.188), calls=%async_computation.9 | async-start | bytes 4194304
  102.2 16.5 %copy-start.16 = (f16[2,224,1024]{2,1,0:T(8,128)(2,1)S(1)}, f16[2,224,1024]{2,1,0:T(8,128)(2,1)}, u32[]{:S(2)}) copy-start(f16[2,224,1024]{2,1,0:T(8,128)(2,1)} %copy-done.15) | copy-start | bytes 2752516
  102.2 25.6 %collective-permute-start.1 = (f16[2,224,1024]{2,1,0:T(8,128)(2,1)}, f16[2,224,1024]{2,1,0:T(8,128)(2,1)S(1)}, u32[]{:S(2)}, u32[]{:S(2)}) collective-permute-start(f16[2,224,1024]{2,1,0:T(8,128)(2,1)} %get-tuple-element.88), channel_id=1, source_target_pairs={{0,1},{4,5},{8,9},{12,13},{16,17},{20,21},{24,25},{28,29}} | collective-permute-start | bytes 2752520 | tf_op jit(solution)/shard_map/ppermute | solution.py:44
  122.7 23.2 %collective-permute-start.2 = (f16[2,224,1024]{2,1,0:T(8,128)(2,1)}, f16[2,224,1024]{2,1,0:T(8,128)(2,1)S(1)}, u32[]{:S(2)}, u32[]{:S(2)}) collective-permute-start(f16[2,224,1024]{2,1,0:T(8,128)(2,1)} %get-tuple-element.98), channel_id=1, source_target_pairs={{0,1},{1,2},{4,5},{5,6},{8,9},{9,10},{12,13},{13,14},{16,17},{17,1... | collective-permute-start | bytes 2752520 | tf_op jit(solution)/shard_map/ppermute | solution.py:44
  124.0 21.9 %collective-permute-start.4 = (f16[2,224,1024]{2,1,0:T(8,128)(2,1)}, f16[2,224,1024]{2,1,0:T(8,128)(2,1)S(1)}, u32[]{:S(2)}, u32[]{:S(2)}) collective-permute-start(f16[2,224,1024]{2,1,0:T(8,128)(2,1)} %get-tuple-element.97), channel_id=1, source_target_pairs={{3,2},{2,1},{7,6},{6,5},{11,10},{10,9},{15,14},{14,13},{19,18},{18... | collective-permute-start | bytes 2752520 | tf_op jit(solution)/shard_map/ppermute | solution.py:45
  124.8 27.1 %collective-permute-start.7 = (f16[2,224,1024]{2,1,0:T(8,128)(2,1)}, f16[2,224,1024]{2,1,0:T(8,128)(2,1)}, u32[]{:S(2)}, u32[]{:S(2)}) collective-permute-start(f16[2,224,1024]{2,1,0:T(8,128)(2,1)} %get-tuple-element.87), channel_id=1, source_target_pairs={{3,2},{7,6},{11,10},{15,14},{19,18},{23,22},{27,26},{31,30}} | collective-permute-start | bytes 2752520 | tf_op jit(solution)/shard_map/ppermute | solution.py:45
  127.8 43.2 %slice-start.4 = ((s8[7340032]{0:T(1024)(128)(4,1)}), s8[4194304]{0:T(1024)(128)(4,1)S(1)}, s32[]{:S(2)}) async-start(s8[7340032]{0:T(1024)(128)(4,1)} %bitcast.206), calls=%async_computation.10 | async-start | bytes 8388608
  127.8 43.2 %slice-start.5 = ((s8[7340032]{0:T(1024)(128)(4,1)}), s8[3145728]{0:T(1024)(128)(4,1)S(1)}, s32[]{:S(2)}) async-start(s8[7340032]{0:T(1024)(128)(4,1)} %bitcast.206), calls=%async_computation.11 | async-start | bytes 6291456
  139.8 15.5 %copy-start = (f16[1024,2,896]{0,2,1:T(8,128)(2,1)}, f16[1024,2,896]{0,2,1:T(8,128)(2,1)S(1)}, u32[]{:S(2)}) copy-start(f16[1024,2,896]{0,2,1:T(8,128)(2,1)S(1)} %fusion.25) | copy-start | bytes 11010052
  139.8 12.1 %copy-start.6 = (f16[1024,2,896]{0,2,1:T(8,128)(2,1)S(1)}, f16[1024,2,896]{0,2,1:T(8,128)(2,1)}, u32[]{:S(2)}) copy-start(f16[1024,2,896]{0,2,1:T(8,128)(2,1)} %copy-done.5) | copy-start | bytes 11010052
  145.9 25.1 %collective-permute-start.5 = (f16[2,224,1024]{2,1,0:T(8,128)(2,1)S(1)}, f16[2,224,1024]{2,1,0:T(8,128)(2,1)S(1)}, u32[]{:S(2)}, u32[]{:S(2)}) collective-permute-start(f16[2,224,1024]{2,1,0:T(8,128)(2,1)S(1)} %get-tuple-element.38), channel_id=1, source_target_pairs={{0,1},{4,5},{8,9},{12,13},{16,17},{20,21},{24,25},{28,29}} | collective-permute-start | bytes 2752520 | tf_op jit(solution)/shard_map/ppermute | solution.py:44
  150.2 34.4 %collective-permute-start.6 = (f16[2,224,1024]{2,1,0:T(8,128)(2,1)S(1)}, f16[2,224,1024]{2,1,0:T(8,128)(2,1)}, u32[]{:S(2)}, u32[]{:S(2)}) collective-permute-start(f16[2,224,1024]{2,1,0:T(8,128)(2,1)S(1)} %get-tuple-element.40), channel_id=1, source_target_pairs={{3,2},{7,6},{11,10},{15,14},{19,18},{23,22},{27,26},{31,30}} | collective-permute-start | bytes 2752520 | tf_op jit(solution)/shard_map/ppermute | solution.py:45
  155.3 40.5 %collective-permute-start.8 = (f16[2,224,1024]{2,1,0:T(8,128)(2,1)}, f16[2,224,1024]{2,1,0:T(8,128)(2,1)S(1)}, u32[]{:S(2)}, u32[]{:S(2)}) collective-permute-start(f16[2,224,1024]{2,1,0:T(8,128)(2,1)} %get-tuple-element.43), channel_id=1, source_target_pairs={{0,1},{1,2},{4,5},{5,6},{8,9},{9,10},{12,13},{13,14},{16,17},{17,1... | collective-permute-start | bytes 2752520 | tf_op jit(solution)/shard_map/ppermute | solution.py:44
  156.6 43.9 %collective-permute-start.9 = (f16[2,224,1024]{2,1,0:T(8,128)(2,1)}, f16[2,224,1024]{2,1,0:T(8,128)(2,1)}, u32[]{:S(2)}, u32[]{:S(2)}) collective-permute-start(f16[2,224,1024]{2,1,0:T(8,128)(2,1)} %get-tuple-element.44), channel_id=1, source_target_pairs={{3,2},{2,1},{7,6},{6,5},{11,10},{10,9},{15,14},{14,13},{19,18},{18... | collective-permute-start | bytes 2752520 | tf_op jit(solution)/shard_map/ppermute | solution.py:45
  171.0 10.0 %copy-start.13 = (f16[2,224,1024]{2,1,0:T(8,128)(2,1)}, f16[2,224,1024]{2,1,0:T(8,128)(2,1)S(1)}, u32[]{:S(2)}) copy-start(f16[2,224,1024]{2,1,0:T(8,128)(2,1)S(1)} %collective-permute-done.5) | copy-start | bytes 2752516
  184.6 25.8 %collective-permute-start.15 = (f16[2,224,1024]{2,1,0:T(8,128)(2,1)}, f16[2,224,1024]{2,1,0:T(8,128)(2,1)}, u32[]{:S(2)}, u32[]{:S(2)}) collective-permute-start(f16[2,224,1024]{2,1,0:T(8,128)(2,1)} %get-tuple-element.49), channel_id=1, source_target_pairs={{0,1},{4,5},{8,9},{12,13},{16,17},{20,21},{24,25},{28,29}} | collective-permute-start | bytes 2752520 | tf_op jit(solution)/shard_map/ppermute | solution.py:44
  190.0 20.4 %collective-permute-start.16 = (f16[2,224,1024]{2,1,0:T(8,128)(2,1)}, f16[2,224,1024]{2,1,0:T(8,128)(2,1)}, u32[]{:S(2)}, u32[]{:S(2)}) collective-permute-start(f16[2,224,1024]{2,1,0:T(8,128)(2,1)} %get-tuple-element.50), channel_id=1, source_target_pairs={{3,2},{7,6},{11,10},{15,14},{19,18},{23,22},{27,26},{31,30}} | collective-permute-start | bytes 2752520 | tf_op jit(solution)/shard_map/ppermute | solution.py:45
  191.6 5.5 %copy-start.1 = (f16[1024,2,896]{0,2,1:T(8,128)(2,1)S(1)}, f16[1024,2,896]{0,2,1:T(8,128)(2,1)}, u32[]{:S(2)}) copy-start(f16[1024,2,896]{0,2,1:T(8,128)(2,1)} %copy-done) | copy-start | bytes 11010052
  191.6 5.5 %copy-start.14 = (f16[2,224,1024]{2,1,0:T(8,128)(2,1)S(1)}, f16[2,224,1024]{2,1,0:T(8,128)(2,1)}, u32[]{:S(2)}) copy-start(f16[2,224,1024]{2,1,0:T(8,128)(2,1)} %copy-done.13) | copy-start | bytes 2752516
  194.2 16.2 %copy-start.3 = (f16[1024,2,896]{0,2,1:T(8,128)(2,1)S(1)}, f16[1024,2,896]{0,2,1:T(8,128)(2,1)}, u32[]{:S(2)}) copy-start(f16[1024,2,896]{0,2,1:T(8,128)(2,1)} %copy-done.2) | copy-start | bytes 11010052
  194.2 35.8 %collective-permute-start.19 = (f16[2,224,1024]{2,1,0:T(8,128)(2,1)S(1)}, f16[2,224,1024]{2,1,0:T(8,128)(2,1)S(1)}, u32[]{:S(2)}, u32[]{:S(2)}) collective-permute-start(f16[2,224,1024]{2,1,0:T(8,128)(2,1)S(1)} %get-tuple-element.57), channel_id=1, source_target_pairs={{0,1},{1,2},{2,3},{4,5},{5,6},{6,7},{8,9},{9,10},{10,11},{12,13},{... | collective-permute-start | bytes 2752520 | tf_op jit(solution)/shard_map/ppermute | solution.py:44
  195.8 34.2 %collective-permute-start.20 = (f16[2,224,1024]{2,1,0:T(8,128)(2,1)S(1)}, f16[2,224,1024]{2,1,0:T(8,128)(2,1)S(1)}, u32[]{:S(2)}, u32[]{:S(2)}) collective-permute-start(f16[2,224,1024]{2,1,0:T(8,128)(2,1)S(1)} %get-tuple-element.58), channel_id=1, source_target_pairs={{3,2},{2,1},{1,0},{7,6},{6,5},{5,4},{11,10},{10,9},{9,8},{15,14},{... | collective-permute-start | bytes 2752520 | tf_op jit(solution)/shard_map/ppermute | solution.py:45
  200.5 20.5 %copy-start.7 = (f16[1024,2,896]{0,2,1:T(8,128)(2,1)S(1)}, f16[1024,2,896]{0,2,1:T(8,128)(2,1)}, u32[]{:S(2)}) copy-start(f16[1024,2,896]{0,2,1:T(8,128)(2,1)} %copy-done.5) | copy-start | bytes 11010052
  214.0 35.7 %collective-permute-start.17 = (f16[2,224,1024]{2,1,0:T(8,128)(2,1)}, f16[2,224,1024]{2,1,0:T(8,128)(2,1)}, u32[]{:S(2)}, u32[]{:S(2)}) collective-permute-start(f16[2,224,1024]{2,1,0:T(8,128)(2,1)} %get-tuple-element.51), channel_id=1, source_target_pairs={{0,1},{1,2},{4,5},{5,6},{8,9},{9,10},{12,13},{13,14},{16,17},{17,1... | collective-permute-start | bytes 2752520 | tf_op jit(solution)/shard_map/ppermute | solution.py:44
  219.4 30.3 %collective-permute-start.18 = (f16[2,224,1024]{2,1,0:T(8,128)(2,1)}, f16[2,224,1024]{2,1,0:T(8,128)(2,1)}, u32[]{:S(2)}, u32[]{:S(2)}) collective-permute-start(f16[2,224,1024]{2,1,0:T(8,128)(2,1)} %get-tuple-element.52), channel_id=1, source_target_pairs={{3,2},{2,1},{7,6},{6,5},{11,10},{10,9},{15,14},{14,13},{19,18},{18... | collective-permute-start | bytes 2752520 | tf_op jit(solution)/shard_map/ppermute | solution.py:45
  230.0 36.9 %collective-permute-start.21 = (f16[2,224,1024]{2,1,0:T(8,128)(2,1)}, f16[2,224,1024]{2,1,0:T(8,128)(2,1)S(1)}, u32[]{:S(2)}, u32[]{:S(2)}) collective-permute-start(f16[2,224,1024]{2,1,0:T(8,128)(2,1)} %get-tuple-element.59), channel_id=1, source_target_pairs={{0,1},{1,2},{2,3},{4,5},{5,6},{6,7},{8,9},{9,10},{10,11},{12,13},{... | collective-permute-start | bytes 2752520 | tf_op jit(solution)/shard_map/ppermute | solution.py:44
  234.4 32.5 %collective-permute-start.22 = (f16[2,224,1024]{2,1,0:T(8,128)(2,1)}, f16[2,224,1024]{2,1,0:T(8,128)(2,1)}, u32[]{:S(2)}, u32[]{:S(2)}) collective-permute-start(f16[2,224,1024]{2,1,0:T(8,128)(2,1)} %get-tuple-element.60), channel_id=1, source_target_pairs={{3,2},{2,1},{1,0},{7,6},{6,5},{5,4},{11,10},{10,9},{9,8},{15,14},{... | collective-permute-start | bytes 2752520 | tf_op jit(solution)/shard_map/ppermute | solution.py:45
  235.9 13.9 %copy-start.4 = (f16[1024,2,896]{0,2,1:T(8,128)(2,1)S(1)}, f16[1024,2,896]{0,2,1:T(8,128)(2,1)}, u32[]{:S(2)}) copy-start(f16[1024,2,896]{0,2,1:T(8,128)(2,1)} %copy-done.2) | copy-start | bytes 11010052
  270.0 11.8 %collective-permute-start.26 = (bf16[224,1024]{1,0:T(8,128)(2,1)S(1)}, bf16[224,1024]{1,0:T(8,128)(2,1)S(1)}, u32[]{:S(2)}, u32[]{:S(2)}) collective-permute-start(bf16[224,1024]{1,0:T(8,128)(2,1)S(1)} %multiply_convert_fusion.1), channel_id=1, source_target_pairs={{0,1},{1,2},{2,3},{4,5},{5,6},{6,7},{8,9},{9,10},{10,11},{12,13},{... | collective-permute-start | bytes 1376264 | tf_op jit(solution)/shard_map/ppermute | solution.py:58
  274.3 11.6 %collective-permute-start.29 = (bf16[224,1024]{1,0:T(8,128)(2,1)S(1)}, bf16[224,1024]{1,0:T(8,128)(2,1)S(1)}, u32[]{:S(2)}, u32[]{:S(2)}) collective-permute-start(bf16[224,1024]{1,0:T(8,128)(2,1)S(1)} %multiply_convert_fusion.1), channel_id=1, source_target_pairs={{1,0},{2,1},{3,2},{5,4},{6,5},{7,6},{9,8},{10,9},{11,10},{13,12},{... | collective-permute-start | bytes 1376264 | tf_op jit(solution)/shard_map/ppermute | solution.py:60
  281.8 5.4 %collective-permute-start.27 = (bf16[224,1024]{1,0:T(8,128)(2,1)S(1)}, bf16[224,1024]{1,0:T(8,128)(2,1)}, u32[]{:S(2)}, u32[]{:S(2)}) collective-permute-start(bf16[224,1024]{1,0:T(8,128)(2,1)S(1)} %collective-permute-done.26), channel_id=1, source_target_pairs={{1,2},{2,3},{5,6},{6,7},{9,10},{10,11},{13,14},{14,15},{17,18},{18... | collective-permute-start | bytes 1376264 | tf_op jit(solution)/shard_map/ppermute | solution.py:58
  285.9 10.8 %collective-permute-start.30 = (bf16[224,1024]{1,0:T(8,128)(2,1)S(1)}, bf16[224,1024]{1,0:T(8,128)(2,1)S(1)}, u32[]{:S(2)}, u32[]{:S(2)}) collective-permute-start(bf16[224,1024]{1,0:T(8,128)(2,1)S(1)} %collective-permute-done.29), channel_id=1, source_target_pairs={{1,0},{2,1},{5,4},{6,5},{9,8},{10,9},{13,12},{14,13},{17,16},{18,1... | collective-permute-start | bytes 1376264 | tf_op jit(solution)/shard_map/ppermute | solution.py:60
  287.2 10.8 %collective-permute-start.28 = (bf16[224,1024]{1,0:T(8,128)(2,1)}, bf16[224,1024]{1,0:T(8,128)(2,1)}, u32[]{:S(2)}, u32[]{:S(2)}) collective-permute-start(bf16[224,1024]{1,0:T(8,128)(2,1)} %collective-permute-done.27), channel_id=1, source_target_pairs={{2,3},{6,7},{10,11},{14,15},{18,19},{22,23},{26,27},{30,31}} | collective-permute-start | bytes 1376264 | tf_op jit(solution)/shard_map/ppermute | solution.py:58
  296.7 10.4 %collective-permute-start.31 = (bf16[224,1024]{1,0:T(8,128)(2,1)S(1)}, bf16[224,1024]{1,0:T(8,128)(2,1)S(1)}, u32[]{:S(2)}, u32[]{:S(2)}) collective-permute-start(bf16[224,1024]{1,0:T(8,128)(2,1)S(1)} %collective-permute-done.30), channel_id=1, source_target_pairs={{1,0},{5,4},{9,8},{13,12},{17,16},{21,20},{25,24},{29,28}} | collective-permute-start | bytes 1376264 | tf_op jit(solution)/shard_map/ppermute | solution.py:60
  307.1 17.0 %copy-start.10 = (f16[2,224,1024]{2,1,0:T(8,128)(2,1)S(1)}, f16[2,224,1024]{2,1,0:T(8,128)(2,1)}, u32[]{:S(2)}) copy-start(f16[2,224,1024]{2,1,0:T(8,128)(2,1)} %get-tuple-element.45) | copy-start | bytes 2752516
  307.1 25.5 %copy-start.9 = (f16[2,224,1024]{2,1,0:T(8,128)(2,1)S(1)}, f16[2,224,1024]{2,1,0:T(8,128)(2,1)}, u32[]{:S(2)}) copy-start(f16[2,224,1024]{2,1,0:T(8,128)(2,1)} %get-tuple-element.46) | copy-start | bytes 2752516
  308.6 101.8 %all-gather.17.cloned.1.call-start = ((), (), s32[]{:S(2)}) async-start(), calls=%async_computation.5 | async-start | bytes 5505024 | tf_op jit(solution)/shard_map/all_gather | solution.py:115
  309.1 7.4 %collective-permute-start.32 = (bf16[224,1024]{1,0:T(8,128)(2,1)S(1)}, bf16[224,1024]{1,0:T(8,128)(2,1)S(1)}, u32[]{:S(2)}, u32[]{:S(2)}) collective-permute-start(bf16[224,1024]{1,0:T(8,128)(2,1)S(1)} %multiply_convert_fusion), channel_id=1, source_target_pairs={{0,1},{1,2},{2,3},{4,5},{5,6},{6,7},{8,9},{9,10},{10,11},{12,13},{... | collective-permute-start | bytes 1376264 | tf_op jit(solution)/shard_map/ppermute | solution.py:58
  310.6 11.6 %collective-permute-start.35 = (bf16[224,1024]{1,0:T(8,128)(2,1)S(1)}, bf16[224,1024]{1,0:T(8,128)(2,1)S(1)}, u32[]{:S(2)}, u32[]{:S(2)}) collective-permute-start(bf16[224,1024]{1,0:T(8,128)(2,1)S(1)} %multiply_convert_fusion), channel_id=1, source_target_pairs={{1,0},{2,1},{3,2},{5,4},{6,5},{7,6},{9,8},{10,9},{11,10},{13,12},{... | collective-permute-start | bytes 1376264 | tf_op jit(solution)/shard_map/ppermute | solution.py:60
  316.5 6.9 %collective-permute-start.33 = (bf16[224,1024]{1,0:T(8,128)(2,1)S(1)}, bf16[224,1024]{1,0:T(8,128)(2,1)S(1)}, u32[]{:S(2)}, u32[]{:S(2)}) collective-permute-start(bf16[224,1024]{1,0:T(8,128)(2,1)S(1)} %collective-permute-done.32), channel_id=1, source_target_pairs={{1,2},{2,3},{5,6},{6,7},{9,10},{10,11},{13,14},{14,15},{17,18},{18... | collective-permute-start | bytes 1376264 | tf_op jit(solution)/shard_map/ppermute | solution.py:58
  322.2 12.0 %collective-permute-start.36 = (bf16[224,1024]{1,0:T(8,128)(2,1)S(1)}, bf16[224,1024]{1,0:T(8,128)(2,1)S(1)}, u32[]{:S(2)}, u32[]{:S(2)}) collective-permute-start(bf16[224,1024]{1,0:T(8,128)(2,1)S(1)} %collective-permute-done.35), channel_id=1, source_target_pairs={{1,0},{2,1},{5,4},{6,5},{9,8},{10,9},{13,12},{14,13},{17,16},{18,1... | collective-permute-start | bytes 1376264 | tf_op jit(solution)/shard_map/ppermute | solution.py:60
  323.5 12.0 %collective-permute-start.34 = (bf16[224,1024]{1,0:T(8,128)(2,1)S(1)}, bf16[224,1024]{1,0:T(8,128)(2,1)S(1)}, u32[]{:S(2)}, u32[]{:S(2)}) collective-permute-start(bf16[224,1024]{1,0:T(8,128)(2,1)S(1)} %collective-permute-done.33), channel_id=1, source_target_pairs={{2,3},{6,7},{10,11},{14,15},{18,19},{22,23},{26,27},{30,31}} | collective-permute-start | bytes 1376264 | tf_op jit(solution)/shard_map/ppermute | solution.py:58
  324.2 26.2 %collective-permute-start.10 = (f16[2,224,1024]{2,1,0:T(8,128)(2,1)S(1)}, f16[2,224,1024]{2,1,0:T(8,128)(2,1)}, u32[]{:S(2)}, u32[]{:S(2)}) collective-permute-start(f16[2,224,1024]{2,1,0:T(8,128)(2,1)S(1)} %copy-done.10), channel_id=1, source_target_pairs={{0,1},{1,2},{4,5},{5,6},{8,9},{9,10},{12,13},{13,14},{16,17},{17,1... | collective-permute-start | bytes 2752520 | tf_op jit(solution)/shard_map/ppermute | solution.py:44
  332.6 17.8 %collective-permute-start.11 = (f16[2,224,1024]{2,1,0:T(8,128)(2,1)S(1)}, f16[2,224,1024]{2,1,0:T(8,128)(2,1)}, u32[]{:S(2)}, u32[]{:S(2)}) collective-permute-start(f16[2,224,1024]{2,1,0:T(8,128)(2,1)S(1)} %copy-done.9), channel_id=1, source_target_pairs={{3,2},{2,1},{7,6},{6,5},{11,10},{10,9},{15,14},{14,13},{19,18},{18... | collective-permute-start | bytes 2752520 | tf_op jit(solution)/shard_map/ppermute | solution.py:45
  334.2 14.6 %collective-permute-start.37 = (bf16[224,1024]{1,0:T(8,128)(2,1)S(1)}, bf16[224,1024]{1,0:T(8,128)(2,1)S(1)}, u32[]{:S(2)}, u32[]{:S(2)}) collective-permute-start(bf16[224,1024]{1,0:T(8,128)(2,1)S(1)} %collective-permute-done.36), channel_id=1, source_target_pairs={{1,0},{5,4},{9,8},{13,12},{17,16},{21,20},{25,24},{29,28}} | collective-permute-start | bytes 1376264 | tf_op jit(solution)/shard_map/ppermute | solution.py:60
  350.3 15.9 %copy-start.11 = (f16[2,224,1024]{2,1,0:T(8,128)(2,1)S(1)}, f16[2,224,1024]{2,1,0:T(8,128)(2,1)}, u32[]{:S(2)}) copy-start(f16[2,224,1024]{2,1,0:T(8,128)(2,1)} %get-tuple-element.62) | copy-start | bytes 2752516
  350.3 95.5 %all-gather.11.cloned.1.call-start = ((), (), s32[]{:S(2)}) async-start(), calls=%async_computation.2 | async-start | bytes 2293760 | tf_op jit(solution)/shard_map/all_gather | solution.py:123
  350.4 11.2 %copy-start.12 = (f16[2,224,1024]{2,1,0:T(8,128)(2,1)S(1)}, f16[2,224,1024]{2,1,0:T(8,128)(2,1)}, u32[]{:S(2)}) copy-start(f16[2,224,1024]{2,1,0:T(8,128)(2,1)} %get-tuple-element.61) | copy-start | bytes 2752516
  353.5 26.4 %collective-permute-start.12 = (f16[2,224,1024]{2,1,0:T(8,128)(2,1)S(1)}, f16[2,224,1024]{2,1,0:T(8,128)(2,1)S(1)}, u32[]{:S(2)}, u32[]{:S(2)}) collective-permute-start(f16[2,224,1024]{2,1,0:T(8,128)(2,1)S(1)} %get-tuple-element.47), channel_id=1, source_target_pairs={{0,1},{1,2},{2,3},{4,5},{5,6},{6,7},{8,9},{9,10},{10,11},{12,13},{... | collective-permute-start | bytes 2752520 | tf_op jit(solution)/shard_map/ppermute | solution.py:44
  360.3 23.8 %collective-permute-start.13 = (f16[2,224,1024]{2,1,0:T(8,128)(2,1)S(1)}, f16[2,224,1024]{2,1,0:T(8,128)(2,1)S(1)}, u32[]{:S(2)}, u32[]{:S(2)}) collective-permute-start(f16[2,224,1024]{2,1,0:T(8,128)(2,1)S(1)} %get-tuple-element.48), channel_id=1, source_target_pairs={{3,2},{2,1},{1,0},{7,6},{6,5},{5,4},{11,10},{10,9},{9,8},{15,14},{... | collective-permute-start | bytes 2752520 | tf_op jit(solution)/shard_map/ppermute | solution.py:45
  361.6 28.1 %collective-permute-start.23 = (f16[2,224,1024]{2,1,0:T(8,128)(2,1)S(1)}, f16[2,224,1024]{2,1,0:T(8,128)(2,1)S(1)}, u32[]{:S(2)}, u32[]{:S(2)}) collective-permute-start(f16[2,224,1024]{2,1,0:T(8,128)(2,1)S(1)} %copy-done.12), channel_id=1, source_target_pairs={{0,1},{1,2},{2,3},{4,5},{5,6},{6,7},{8,9},{9,10},{10,11},{12,13},{... | collective-permute-start | bytes 2752520 | tf_op jit(solution)/shard_map/ppermute | solution.py:44
  366.2 27.7 %collective-permute-start.24 = (f16[2,224,1024]{2,1,0:T(8,128)(2,1)S(1)}, f16[2,224,1024]{2,1,0:T(8,128)(2,1)S(1)}, u32[]{:S(2)}, u32[]{:S(2)}) collective-permute-start(f16[2,224,1024]{2,1,0:T(8,128)(2,1)S(1)} %copy-done.11), channel_id=1, source_target_pairs={{3,2},{2,1},{1,0},{7,6},{6,5},{5,4},{11,10},{10,9},{9,8},{15,14},{... | collective-permute-start | bytes 2752520 | tf_op jit(solution)/shard_map/ppermute | solution.py:45
  396.7 0.7 collective-permute-start.14
  398.2 75.0 %all-gather.13.cloned.1.call-start = ((), (), s32[]{:S(2)}) async-start(), calls=%async_computation.3 | async-start | bytes 2293760 | tf_op jit(solution)/shard_map/all_gather | solution.py:123
  398.7 0.9 collective-permute-start.25
  (5 other events, 6.1 us)
Sparse Core Ops, SparseCore 0:
  9.2 39.4 all-gather.8
  50.6 36.7 all-gather.6
  308.7 49.3 all-gather.14
  359.6 50.8 all-gather.16
  411.9 33.9 all-gather.10
  447.2 25.9 all-gather.12
